TPU v7x, 128 devices: a whole 4x4x4 slice. The times are simulated.
128 devices in a mesh: ia: 4 (over x_lo, core), ja: 16 (over z, y), ka: 2 (over x_hi).
Axes of the slice: x: 4 (x_hi: 2, x_lo: 2; x = x_hi * 2 + x_lo), y: 4, z: 4, core: 2. Of those that a mesh axis runs over, the one named last changes fastest.
Arguments:
- tensor: bfloat16 [1024, 2048, 512], P('ia', 'ja', 'ka'), may hold values from -6000 to 6000
- factor_b: float32 [2048, 256], P('ja'), may hold values from 0.1 to 1
- factor_c: float32 [512, 256], P('ka'), may hold values from 0.1 to 1
Outputs:
- factor_a: float32 [1024, 256], P('ia')
- refit_b: float32 [2048, 256], P('ja')
- refit_c: float32 [512, 256], P('ka')
All inputs are finite; a program needn't handle non-finite values.
Results may differ from a plain program's by a relative error of at most 0.009.
Values sent between devices are 32-bit elements; how exact they have to be, the bound alone decides.
No kernel may reach another device: no remote copies, remote signals or barrier semaphores. Data moves between devices by JAX's collectives and lax.ppermute only.
A program may use at most 128 MiB of HBM per device.

v0:
```python
import functools

import jax
import jax.numpy as jnp
from jax import lax
from jax.experimental import pallas as pl
from jax.experimental.pallas import tpu as pltpu
from jax.sharding import PartitionSpec as P

eps = 1e-06
PANEL = 32


def gram_of(matrix):
    return jnp.dot(
        matrix.T, matrix, precision=lax.Precision.HIGHEST, preferred_element_type=jnp.float32
    )


def product(rows, square):
    return jnp.dot(
        rows, square, precision=lax.Precision.HIGHEST, preferred_element_type=jnp.float32
    )


def reciprocal(x):
    r = pl.reciprocal(x, approx=True)
    r = r * (2.0 - x * r)
    return r * (2.0 - x * r)


def sweep(a, n):
    for k in range(0, n, 2):
        p, q, r = a[k][k], a[k + 1][k], a[k + 1][k + 1]
        d = reciprocal(p * r - q * q)
        ip, iq, ir = r * d, -(q * d), p * d
        c0 = [a[max(i, k)][min(i, k)] for i in range(n)]
        c1 = [a[max(i, k + 1)][min(i, k + 1)] for i in range(n)]
        b0 = [c0[i] * ip + c1[i] * iq for i in range(n)]
        b1 = [c0[i] * iq + c1[i] * ir for i in range(n)]
        rest = [i for i in range(n) if i not in (k, k + 1)]
        for i in rest:
            for j in rest:
                if j <= i:
                    a[i][j] = a[i][j] - (b0[i] * c0[j] + b1[i] * c1[j])
        for i in rest:
            a[max(i, k)][min(i, k)] = b0[i]
            a[max(i, k + 1)][min(i, k + 1)] = b1[i]
        a[k][k], a[k + 1][k], a[k + 1][k + 1] = -ip, -iq, -ir
    return a


def total_of(terms):
    while len(terms) > 1:
        terms = [terms[2 * i] + terms[2 * i + 1] for i in range(len(terms) // 2)]
    return terms[0]


def eliminate(w, first, last):
    n = w.shape[0]
    tiles, groups = n // 128, PANEL // 8
    sub = lax.broadcasted_iota(jnp.int32, (8, 128), 0)
    lane = lax.broadcasted_iota(jnp.int32, (8, 128), 1)

    def step(p, carry):
        x = [
            [w[8 * g : 8 * g + 8, 128 * h : 128 * h + 128] for h in range(tiles)]
            for g in range(groups)
        ]
        old = w[0:PANEL, :]
        for q in range(groups):
            l = 8 * q
            inside = (lane >= l) & (lane < l + 8)
            columns = [
                [jnp.broadcast_to(x[g][0][:, l + j : l + j + 1], (8, 128)) for j in range(8)]
                for g in range(groups)
            ]
            a = [
                [jnp.broadcast_to(columns[q][j][i : i + 1, :], (8, 128)) for j in range(i + 1)]
                for i in range(8)
            ]
            a = sweep(a, 8)
            inverse = []
            for j in range(8):
                column = a[7][j]
                for i in range(7):
                    column = jnp.where(sub == i, a[max(i, j)][min(i, j)], column)
                inverse.append(column)
            source = list(x[q])
            source[0] = jnp.where(inside, (lane - l == sub).astype(jnp.float32), source[0])
            x[q] = [
                -total_of(
                    [
                        inverse[j] * jnp.broadcast_to(source[h][j : j + 1, :], (8, 128))
                        for j in range(8)
                    ]
                )
                for h in range(tiles)
            ]
            rows = [
                [jnp.broadcast_to(x[q][h][j : j + 1, :], (8, 128)) for j in range(8)]
                for h in range(tiles)
            ]
            for g in range(groups):
                if g == q:
                    continue
                for h in range(tiles):
                    base = jnp.where(inside, 0.0, x[g][h]) if h == 0 else x[g][h]
                    x[g][h] = base - total_of([columns[g][j] * rows[h][j] for j in range(8)])
        panel = jnp.concatenate([jnp.concatenate(x[g], axis=1) for g in range(groups)], axis=0)
        place = lax.broadcasted_iota(jnp.int32, (PANEL, n), 1)
        across = jnp.where(place >= n - PANEL * p, -old, old)
        update = lax.dot_general(
            across,
            panel,
            (((0,), (0,)), ((), ())),
            precision=lax.Precision.HIGHEST,
            preferred_element_type=jnp.float32,
        )
        place = lax.broadcasted_iota(jnp.int32, (n - PANEL, n), 1)
        rest = jnp.where(place < PANEL, 0.0, w[PANEL:, :]) - update[PANEL:, :]
        w[0 : n - PANEL, :] = pltpu.roll(rest, n - PANEL, 1)
        w[n - PANEL :, :] = pltpu.roll(panel, n - PANEL, 1)
        return carry

    lax.fori_loop(first, last, step, 0)


def mixed_of(one_ref, two_ref):
    mixed = one_ref[...] * two_ref[...]
    row = lax.broadcasted_iota(jnp.int32, mixed.shape, 0)
    column = lax.broadcasted_iota(jnp.int32, mixed.shape, 1)
    diagonal = jnp.where(row == column, mixed, 0.0)
    down = lax.rsqrt(jnp.sum(diagonal, axis=1, keepdims=True))
    along = lax.rsqrt(jnp.sum(diagonal, axis=0, keepdims=True))
    return mixed, down, along


def inverse_kernel(first, last, one_ref, two_ref, *rest):
    out_ref = rest[-1]
    mixed, down, along = mixed_of(one_ref, two_ref)
    out_ref[...] = mixed * down * along if first == 0 else rest[0][...]
    eliminate(out_ref, first, last)
    if last == out_ref.shape[0] // PANEL:
        out_ref[...] = out_ref[...] * down * along


def inverse_of(one, two, first=0, last=None, state=()):
    n = one.shape[0]
    last = n // PANEL if last is None else last
    whole = pl.BlockSpec(memory_space=pltpu.VMEM)
    return pl.pallas_call(
        functools.partial(inverse_kernel, first, last),
        out_shape=jax.ShapeDtypeStruct((n, n), jnp.float32),
        in_specs=[whole] * (2 + len(state)),
        out_specs=whole,
        compiler_params=pltpu.CompilerParams(vmem_limit_bytes=6 << 20),
        cost_estimate=pl.CostEstimate(
            flops=(last - first) << 31, bytes_accessed=12 * n * n, transcendentals=0
        ),
        name="inverse",
    )(one, two, *state)


def scatter_sum(x, axes):
    n = lax.axis_size(axes)
    pieces = x.reshape(n, x.shape[0] // n, x.shape[1])
    return jnp.sum(lax.all_to_all(pieces, axes, 0, 0), axis=0)


def gather_rows(x, axes):
    n = lax.axis_size(axes)
    copies = jnp.broadcast_to(x[None], (n,) + x.shape)
    return lax.all_to_all(copies, axes, 0, 0).reshape(n * x.shape[0], x.shape[1])


def add_partner(x, axis, step):
    n = lax.axis_size(axis)
    return x + lax.ppermute(x, axis, [(i, i ^ step) for i in range(n)])


def sum_along(x, axis):
    side, parts = 4, []
    for s in range(1, side):
        pairs = []
        for i in range(side * side):
            place = [i // side, i % side]
            place[axis] = (place[axis] + s) % side
            pairs.append((i, place[0] * side + place[1]))
        parts.append(lax.ppermute(x, "ja", pairs))
    return (x + parts[1]) + (parts[0] + parts[2])


def diagonal_of(square):
    n = square.shape[0]
    return jnp.sum(jnp.where(jnp.eye(n, dtype=bool), square, 0.0), axis=0)


CHUNK = 32
AHEAD = 3


def over_chunks(t_ref, held_ref, sems, use, ready=lambda: None):
    rows, cols, deep = held_ref.shape
    chunks = rows // CHUNK

    def copy(q):
        part = pl.ds(q * CHUNK, CHUNK)
        return pltpu.make_async_copy(t_ref.at[part], held_ref.at[part], sems.at[q])

    for q in range(AHEAD):
        copy(q).start()
    ready()

    @pl.loop(0, chunks)
    def _(q):
        copy(q).wait()

        @pl.when(q + AHEAD < chunks)
        def _():
            copy(q + AHEAD).start()

        part = pl.ds(pl.multiple_of(q * CHUNK, CHUNK), CHUNK)
        use(part, held_ref[part].reshape(CHUNK * cols, deep))


def inner_of(flat, c_ref):
    inner = jnp.dot(flat, c_ref[...].astype(jnp.bfloat16), preferred_element_type=jnp.float32)
    return inner.reshape(CHUNK, flat.shape[0] // CHUNK, c_ref.shape[1])


def first_kernel(t_ref, b_ref, c_ref, out_ref, held_ref, sems, b_held, c_held, b_sem, c_sem):
    b_copy = pltpu.make_async_copy(b_ref, b_held, b_sem)
    c_copy = pltpu.make_async_copy(c_ref, c_held, c_sem)
    b_copy.start()
    c_copy.start()

    def use(part, flat):
        out_ref[part, :] = jnp.sum(inner_of(flat, c_held) * b_held[...][None], axis=1)

    def ready():
        b_copy.wait()
        c_copy.wait()

    over_chunks(t_ref, held_ref, sems, use, ready)


def second_kernel(t_ref, a_ref, c_ref, out_ref, held_ref, sems):
    def use(part, flat):
        out_ref[...] += jnp.sum(inner_of(flat, c_ref) * a_ref[part, :][:, None, :], axis=0)

    out_ref[...] = jnp.zeros_like(out_ref)
    over_chunks(t_ref, held_ref, sems, use)


def third_kernel(t_ref, a_ref, b_ref, out_ref, held_ref, sems):
    def use(part, flat):
        paired = (a_ref[part, :][:, None, :] * b_ref[...][None]).astype(jnp.bfloat16)
        out_ref[...] += lax.dot_general(
            flat,
            paired.reshape(flat.shape[0], b_ref.shape[1]),
            (((0,), (0,)), ((), ())),
            preferred_element_type=jnp.float32,
        )

    out_ref[...] = jnp.zeros_like(out_ref)
    over_chunks(t_ref, held_ref, sems, use)


def tensor_pass(kernel, rows, tensor, one, two, name):
    rank = one.shape[1]
    whole = pl.BlockSpec(memory_space=pltpu.VMEM)
    away = pl.BlockSpec(memory_space=pl.ANY)
    fetched = kernel is first_kernel
    small = [pltpu.VMEM(x.shape, x.dtype) for x in (one, two)] if fetched else []
    return pl.pallas_call(
        kernel,
        out_shape=jax.ShapeDtypeStruct((rows, rank), jnp.float32),
        in_specs=[away] + [away if fetched else whole] * 2,
        out_specs=whole,
        scratch_shapes=[
            pltpu.VMEM(tensor.shape, tensor.dtype),
            pltpu.SemaphoreType.DMA((tensor.shape[0] // CHUNK,)),
        ]
        + small
        + [pltpu.SemaphoreType.DMA] * len(small),
        compiler_params=pltpu.CompilerParams(vmem_limit_bytes=(60 if fetched else 48) << 20),
        cost_estimate=pl.CostEstimate(
            flops=2 * tensor.size * rank, bytes_accessed=2 * tensor.size, transcendentals=0
        ),
        name=name,
    )(tensor, one, two)


def local(tensor, factor_b, factor_c):
    rows_i, cols_j, deep_k = tensor.shape
    rank = factor_b.shape[1]
    n_i, n_j, n_k = (lax.axis_size(axis) for axis in ("ia", "ja", "ka"))
    me_i, me_k = lax.axis_index("ia"), lax.axis_index("ka")
    total_i, total_j, total_k = rows_i * n_i, cols_j * n_j, deep_k * n_k
    every = ("ia", "ja", "ka")


    gram_b = sum_along(gram_of(factor_b), 0)
    partial_a = tensor_pass(first_kernel, rows_i, tensor, factor_b, factor_c, "first")
    gram_b, late_c, partial_a = lax.optimization_barrier((gram_b, factor_c, partial_a))
    gram_b = sum_along(gram_b, 1)
    gram_c = add_partner(gram_of(late_c), "ka", 1)
    shared_a = scatter_sum(partial_a, ("ja", "ka"))
    gram_b, gram_c, shared_a = lax.optimization_barrier((gram_b, gram_c, shared_a))
    moment_a = gather_rows(shared_a, every)
    all_a = product(moment_a, inverse_of(gram_b, gram_c))
    raw_gram_a = gram_of(all_a)
    scale_a = jnp.sqrt(diagonal_of(raw_gram_a) / total_i + eps)
    raw_a = lax.dynamic_slice_in_dim(all_a, me_i * rows_i, rows_i, 0)
    factor_a = raw_a / scale_a

    partial_b = tensor_pass(second_kernel, cols_j, tensor, raw_a, factor_c, "second")
    moment_b = jnp.sum(gather_rows(partial_b, ("ia", "ka")).reshape(-1, cols_j, rank), axis=0)
    raw_b = product(moment_b, inverse_of(raw_gram_a, gram_c)) * scale_a
    sums_b = jnp.sum(gather_rows(jnp.sum(raw_b * raw_b, axis=0, keepdims=True), "ja"), axis=0)
    scale_b = jnp.sqrt(sums_b / total_j + eps)
    raw_gram_b = sum_along(gram_of(raw_b), 0)
    scale_b, raw_gram_b = lax.optimization_barrier((scale_b, raw_gram_b))
    raw_gram_b = sum_along(raw_gram_b, 1)
    refit_b = raw_b / scale_b

    partial_c = tensor_pass(third_kernel, deep_k, tensor, factor_a, refit_b, "third")
    raw_gram_b, partial_c = lax.optimization_barrier((raw_gram_b, partial_c))
    shared_c = scatter_sum(partial_c, ("ia", "ja"))
    half = rank // PANEL // 2
    state = inverse_of(raw_gram_a, raw_gram_b, 0, half)
    state, shared_c = lax.optimization_barrier((state, shared_c))
    moment_c = gather_rows(shared_c, every)
    inverse_c = inverse_of(raw_gram_a, raw_gram_b, half, None, (state,))
    both = scale_a * scale_b
    all_c = product(moment_c * both, inverse_c) * both
    scale_c = jnp.sqrt(jnp.sum(all_c * all_c, axis=0) / total_k + eps)
    spread = all_c.reshape(n_i * n_j, n_k, deep_k // (n_i * n_j), rank)
    raw_c = lax.dynamic_index_in_dim(spread, me_k, 1, keepdims=False).reshape(deep_k, rank)
    refit_c = raw_c / scale_c
    return (factor_a, refit_b, refit_c)


def solution(mesh):
    return jax.shard_map(
        local,
        mesh=mesh,
        in_specs=(P("ia", "ja", "ka"), P("ja", None), P("ka", None)),
        out_specs=(P("ia", None), P("ja", None), P("ka", None)),
        check_vma=False,
    )
```

profile of v0, /device:TPU:1, one launch (start us, length us, event | category | flops | bytes accessed | tf_op | source)
XLA Modules:
  0.0 169.8 jit_solution(12555864836554632562)
XLA Ops:
  0.6 1.4 fusion.5
  2.1 4.6 %collective-permute-start.2 = (f32[256,256]{1,0:T(8,128)S(1)}, f32[256,256]{1,0:T(8,128)S(1)}, u32[]{:S(2)}, u32[]{:S(2)}) collective-permute-start(f32[256,256]{1,0:T(8,128)S(1)} %fusion.5), channel_id=1, source_target_pairs={{0,24},{2,26},{4,28},{6,30},{8,0},{10,2},{12,4},{14,6},{16,8},{18,... | collective-permute-start | bytes 786440 | tf_op jit(solution)/shard_map/ppermute | solution.py:190
  6.7 1.3 collective-permute-start
  8.0 8.8 %first.1 = f32[256,256]{1,0:T(8,128)} custom-call(bf16[256,128,256]{2,1,0:T(8,128)(2,1)} %t_ref.5, f32[128,256]{1,0:T(8,128)} %b_ref.1, f32[256,256]{1,0:T(8,128)} %c_ref.3), custom_call_target="tpu_custom_call" | custom-call | flops 4294967296 | bytes 16777216 | tf_op jit(solution)/shard_map/first/pallas_call | solution.py:276
  17.2 1.9 %collective-permute-done = f32[256,256]{1,0:T(8,128)S(1)} collective-permute-done((f32[256,256]{1,0:T(8,128)S(1)}, f32[256,256]{1,0:T(8,128)S(1)}, u32[]{:S(2)}, u32[]{:S(2)}) %collective-permute-start) | collective-permute-done | bytes 262176 | tf_op jit(solution)/shard_map/ppermute | solution.py:190
  19.8 2.8 %collective-permute-start.6 = (f32[256,256]{1,0:T(8,128)S(1)}, f32[256,256]{1,0:T(8,128)S(1)}, u32[]{:S(2)}, u32[]{:S(2)}) collective-permute-start(f32[256,256]{1,0:T(8,128)S(1)} %fusion.6), channel_id=1, source_target_pairs={{0,1},{1,0},{2,3},{3,2},{4,5},{5,4},{6,7},{7,6},{8,9},{9,8},{10,11... | collective-permute-start | bytes 786440 | tf_op jit(solution)/shard_map/ppermute | solution.py:179
  22.6 2.7 %collective-permute-start.5 = (f32[256,256]{1,0:T(8,128)S(1)}, f32[256,256]{1,0:T(8,128)S(1)}, u32[]{:S(2)}, u32[]{:S(2)}) collective-permute-start(f32[256,256]{1,0:T(8,128)S(1)} %add_add_fusion.3), channel_id=1, source_target_pairs={{0,6},{2,0},{4,2},{6,4},{8,14},{10,8},{12,10},{14,12},{16,22},{18,... | collective-permute-start | bytes 786440 | tf_op jit(solution)/shard_map/ppermute | solution.py:190
  25.3 1.6 collective-permute-start.3
  27.0 4.9 %all-to-all-start = ((f32[32,8,256]{2,1,0:T(8,128)}), f32[32,8,256]{2,1,0:T(8,128)S(1)}, u32[]{:S(2)}, u32[]{:S(2)}) async-start(f32[32,8,256]{2,1,0:T(8,128)} %bitcast.16), calls=%async_computation | async-start | bytes 524288 | tf_op jit(solution)/shard_map/all_to_all | solution.py:168
  31.9 10.9 %all-to-all-done = f32[32,8,256]{2,1,0:T(8,128)S(1)} async-done(((f32[32,8,256]{2,1,0:T(8,128)}), f32[32,8,256]{2,1,0:T(8,128)S(1)}, u32[]{:S(2)}, u32[]{:S(2)}) %all-to-all-start) | async-done | bytes 262176 | tf_op jit(solution)/shard_map/all_to_all | solution.py:168
  43.0 1.0 broadcast_in_dim.12
  44.1 6.7 %all-to-all-start.1 = ((f32[128,8,256]{2,1,0:T(8,128)}), f32[128,8,256]{2,1,0:T(8,128)S(1)}, u32[]{:S(2)}, u32[]{:S(2)}) async-start(f32[128,8,256]{2,1,0:T(8,128)} %broadcast_in_dim.12), calls=%async_computation.1 | async-start | bytes 2097152 | tf_op jit(solution)/shard_map/all_to_all | solution.py:174
  50.8 12.8 %inverse.4 = f32[256,256]{1,0:T(8,128)S(1)} custom-call(f32[256,256]{1,0:T(8,128)S(1)} %add_add_fusion.2.one_ref, f32[256,256]{1,0:T(8,128)S(1)} %add.69.two_ref), custom_call_target="tpu_custom_call" | custom-call | flops 17179869184 | bytes 786432 | tf_op jit(solution)/shard_map/inverse/pallas_call | solution.py:152
  63.5 6.9 %all-to-all-done.1 = f32[128,8,256]{2,1,0:T(8,128)S(1)} async-done(((f32[128,8,256]{2,1,0:T(8,128)}), f32[128,8,256]{2,1,0:T(8,128)S(1)}, u32[]{:S(2)}, u32[]{:S(2)}) %all-to-all-start.1) | async-done | bytes 1048608 | tf_op jit(solution)/shard_map/all_to_all | solution.py:174
  71.5 1.9 %select_reduce_fusion = (f32[256]{0:T(256)S(1)}, f32[256,256]{1,0:T(8,128)S(1)}) fusion(f32[1024,256]{1,0:T(8,128)S(1)} %fusion), kind=kOutput, calls=%fused_computation.9 | convolution fusion | flops 805502720 | bytes 1311744 | tf_op jit(solution)/shard_map/dot_general | solution.py:15
  73.4 8.2 %second.1 = f32[128,256]{1,0:T(8,128)S(1)} custom-call(bf16[256,128,256]{2,1,0:T(8,128)(2,1)} %t_ref.5, f32[256,256]{1,0:T(8,128)S(1)} %get-tuple-element.28.a_ref, f32[256,256]{1,0:T(8,128)S(1)} %copy-done), custom_call_target="tpu_custom_call" | custom-call | flops 4294967296 | bytes 16777216 | tf_op jit(solution)/shard_map/second/pallas_call | solution.py:276
  81.6 1.1 broadcast_in_dim.14
  82.6 3.9 %all-to-all-start.2 = ((f32[8,128,256]{2,1,0:T(8,128)}), f32[8,128,256]{2,1,0:T(8,128)S(1)}, u32[]{:S(2)}, u32[]{:S(2)}) async-start(f32[8,128,256]{2,1,0:T(8,128)} %broadcast_in_dim.14), calls=%async_computation.2 | async-start | bytes 2097152 | tf_op jit(solution)/shard_map/all_to_all | solution.py:174
  86.6 12.8 %inverse.5 = f32[256,256]{1,0:T(8,128)S(1)} custom-call(f32[256,256]{1,0:T(8,128)S(1)} %get-tuple-element.30.one_ref, f32[256,256]{1,0:T(8,128)S(1)} %add.69.two_ref), custom_call_target="tpu_custom_call" | custom-call | flops 17179869184 | bytes 786432 | tf_op jit(solution)/shard_map/inverse/pallas_call | solution.py:152
  99.3 2.2 %all-to-all-done.2 = f32[8,128,256]{2,1,0:T(8,128)S(1)} async-done(((f32[8,128,256]{2,1,0:T(8,128)}), f32[8,128,256]{2,1,0:T(8,128)S(1)}, u32[]{:S(2)}, u32[]{:S(2)}) %all-to-all-start.2) | async-done | bytes 1048608 | tf_op jit(solution)/shard_map/all_to_all | solution.py:174
  102.8 1.1 collective-permute-start.8
  105.4 3.6 %all-to-all-start.3 = ((f32[16,1,256]{2,1,0:T(1,128)}), f32[16,1,256]{2,1,0:T(1,128)S(1)}, u32[]{:S(2)}, u32[]{:S(2)}) async-start(f32[16,1,256]{2,1,0:T(1,128)} %broadcast_in_dim.15), calls=%async_computation.3 | async-start | bytes 32768 | tf_op jit(solution)/shard_map/all_to_all | solution.py:174
  109.0 8.6 %all-to-all-done.3 = f32[16,1,256]{2,1,0:T(1,128)S(1)} async-done(((f32[16,1,256]{2,1,0:T(1,128)}), f32[16,1,256]{2,1,0:T(1,128)S(1)}, u32[]{:S(2)}, u32[]{:S(2)}) %all-to-all-start.3) | async-done | bytes 16416 | tf_op jit(solution)/shard_map/all_to_all | solution.py:174
  118.1 1.2 collective-permute-start.11
  119.4 7.8 %third.1 = f32[256,256]{1,0:T(8,128)S(1)} custom-call(bf16[256,128,256]{2,1,0:T(8,128)(2,1)} %t_ref.5, f32[256,256]{1,0:T(8,128)S(1)} %get-tuple-element.27.a_ref, f32[128,256]{1,0:T(8,128)S(1)} %broadcast_divide_fusion.2.b_ref), custom_call_target="tpu_custom_call" | custom-call | flops 4294967296 | bytes 16777216 | tf_op jit(solution)/shard_map/third/pallas_call | solution.py:276
  127.3 2.4 %collective-permute-done.10 = f32[256,256]{1,0:T(8,128)S(1)} collective-permute-done((f32[256,256]{1,0:T(8,128)S(1)}, f32[256,256]{1,0:T(8,128)S(1)}, u32[]{:S(2)}, u32[]{:S(2)}) %collective-permute-start.10) | collective-permute-done | bytes 262176 | tf_op jit(solution)/shard_map/ppermute | solution.py:190
  130.5 8.1 %all-to-all-start.4 = ((f32[64,4,256]{2,1,0:T(4,128)}), f32[64,4,256]{2,1,0:T(4,128)S(1)}, u32[]{:S(2)}, u32[]{:S(2)}) async-start(f32[64,4,256]{2,1,0:T(4,128)} %reshape.46), calls=%async_computation.4 | async-start | bytes 524288 | tf_op jit(solution)/shard_map/all_to_all | solution.py:168
  138.6 6.4 %inverse.6.rest_0_ = f32[256,256]{1,0:T(8,128)S(1)} custom-call(f32[256,256]{1,0:T(8,128)S(1)} %get-tuple-element.30.one_ref, f32[256,256]{1,0:T(8,128)S(1)} %add_add_fusion.two_ref), custom_call_target="tpu_custom_call" | custom-call | flops 8589934592 | bytes 786432 | tf_op jit(solution)/shard_map/inverse/pallas_call | solution.py:152
  145.1 2.9 %all-to-all-done.4 = f32[64,4,256]{2,1,0:T(4,128)S(1)} async-done(((f32[64,4,256]{2,1,0:T(4,128)}), f32[64,4,256]{2,1,0:T(4,128)S(1)}, u32[]{:S(2)}, u32[]{:S(2)}) %all-to-all-start.4) | async-done | bytes 262176 | tf_op jit(solution)/shard_map/all_to_all | solution.py:168
  148.9 5.0 %all-to-all-start.5 = ((f32[128,4,256]{2,1,0:T(4,128)}), f32[128,4,256]{2,1,0:T(4,128)S(1)}, u32[]{:S(2)}, u32[]{:S(2)}) async-start(f32[128,4,256]{2,1,0:T(4,128)} %broadcast_in_dim.16), calls=%async_computation.5 | async-start | bytes 1048576 | tf_op jit(solution)/shard_map/all_to_all | solution.py:174
  153.9 6.4 %inverse.7 = f32[256,256]{1,0:T(8,128)S(1)} custom-call(f32[256,256]{1,0:T(8,128)S(1)} %get-tuple-element.30.one_ref, f32[256,256]{1,0:T(8,128)S(1)} %add_add_fusion.two_ref, f32[256,256]{1,0:T(8,128)S(1)} %inverse.6.rest_0_), custom_call_target="tpu_custom_call" | custom-call | flops 8589934592 | bytes 786432 | tf_op jit(solution)/shard_map/inverse/pallas_call | solution.py:152
  160.4 7.6 %all-to-all-done.5 = f32[128,4,256]{2,1,0:T(4,128)S(1)} async-done(((f32[128,4,256]{2,1,0:T(4,128)}), f32[128,4,256]{2,1,0:T(4,128)S(1)}, u32[]{:S(2)}, u32[]{:S(2)}) %all-to-all-start.5) | async-done | bytes 524320 | tf_op jit(solution)/shard_map/all_to_all | solution.py:174
  (51 shorter events, 9.1 us)
Async XLA Ops:
  0.6 18.5 %copy-start = (f32[256,256]{1,0:T(8,128)S(1)}, f32[256,256]{1,0:T(8,128)}, u32[]{:S(2)}) copy-start(f32[256,256]{1,0:T(8,128)} %c_ref.3) | copy-start | bytes 786436
  2.1 15.1 %collective-permute-start.2 = (f32[256,256]{1,0:T(8,128)S(1)}, f32[256,256]{1,0:T(8,128)S(1)}, u32[]{:S(2)}, u32[]{:S(2)}) collective-permute-start(f32[256,256]{1,0:T(8,128)S(1)} %fusion.5), channel_id=1, source_target_pairs={{0,24},{2,26},{4,28},{6,30},{8,0},{10,2},{12,4},{14,6},{16,8},{18,... | collective-permute-start | bytes 786440 | tf_op jit(solution)/shard_map/ppermute | solution.py:190
  6.7 10.4 %collective-permute-start.1 = (f32[256,256]{1,0:T(8,128)S(1)}, f32[256,256]{1,0:T(8,128)S(1)}, u32[]{:S(2)}, u32[]{:S(2)}) collective-permute-start(f32[256,256]{1,0:T(8,128)S(1)} %fusion.5), channel_id=1, source_target_pairs={{0,8},{2,10},{4,12},{6,14},{8,16},{10,18},{12,20},{14,22},{16,24},... | collective-permute-start | bytes 786440 | tf_op jit(solution)/shard_map/ppermute | solution.py:190
  6.7 12.4 %collective-permute-start = (f32[256,256]{1,0:T(8,128)S(1)}, f32[256,256]{1,0:T(8,128)S(1)}, u32[]{:S(2)}, u32[]{:S(2)}) collective-permute-start(f32[256,256]{1,0:T(8,128)S(1)} %fusion.5), channel_id=1, source_target_pairs={{0,16},{2,18},{4,20},{6,22},{8,24},{10,26},{12,28},{14,30},{16,0},... | collective-permute-start | bytes 786440 | tf_op jit(solution)/shard_map/ppermute | solution.py:190
  19.8 23.1 %collective-permute-start.6 = (f32[256,256]{1,0:T(8,128)S(1)}, f32[256,256]{1,0:T(8,128)S(1)}, u32[]{:S(2)}, u32[]{:S(2)}) collective-permute-start(f32[256,256]{1,0:T(8,128)S(1)} %fusion.6), channel_id=1, source_target_pairs={{0,1},{1,0},{2,3},{3,2},{4,5},{5,4},{6,7},{7,6},{8,9},{9,8},{10,11... | collective-permute-start | bytes 786440 | tf_op jit(solution)/shard_map/ppermute | solution.py:179
  22.6 20.4 %collective-permute-start.5 = (f32[256,256]{1,0:T(8,128)S(1)}, f32[256,256]{1,0:T(8,128)S(1)}, u32[]{:S(2)}, u32[]{:S(2)}) collective-permute-start(f32[256,256]{1,0:T(8,128)S(1)} %add_add_fusion.3), channel_id=1, source_target_pairs={{0,6},{2,0},{4,2},{6,4},{8,14},{10,8},{12,10},{14,12},{16,22},{18,... | collective-permute-start | bytes 786440 | tf_op jit(solution)/shard_map/ppermute | solution.py:190
  25.3 17.6 %collective-permute-start.4 = (f32[256,256]{1,0:T(8,128)S(1)}, f32[256,256]{1,0:T(8,128)S(1)}, u32[]{:S(2)}, u32[]{:S(2)}) collective-permute-start(f32[256,256]{1,0:T(8,128)S(1)} %add_add_fusion.3), channel_id=1, source_target_pairs={{0,2},{2,4},{4,6},{6,0},{8,10},{10,12},{12,14},{14,8},{16,18},{18,... | collective-permute-start | bytes 786440 | tf_op jit(solution)/shard_map/ppermute | solution.py:190
  25.3 17.6 %collective-permute-start.3 = (f32[256,256]{1,0:T(8,128)S(1)}, f32[256,256]{1,0:T(8,128)S(1)}, u32[]{:S(2)}, u32[]{:S(2)}) collective-permute-start(f32[256,256]{1,0:T(8,128)S(1)} %add_add_fusion.3), channel_id=1, source_target_pairs={{0,4},{2,6},{4,0},{6,2},{8,12},{10,14},{12,8},{14,10},{16,20},{18,... | collective-permute-start | bytes 786440 | tf_op jit(solution)/shard_map/ppermute | solution.py:190
  27.0 15.9 %all-to-all-start = ((f32[32,8,256]{2,1,0:T(8,128)}), f32[32,8,256]{2,1,0:T(8,128)S(1)}, u32[]{:S(2)}, u32[]{:S(2)}) async-start(f32[32,8,256]{2,1,0:T(8,128)} %bitcast.16), calls=%async_computation | async-start | bytes 524288 | tf_op jit(solution)/shard_map/all_to_all | solution.py:168
  44.1 26.4 %all-to-all-start.1 = ((f32[128,8,256]{2,1,0:T(8,128)}), f32[128,8,256]{2,1,0:T(8,128)S(1)}, u32[]{:S(2)}, u32[]{:S(2)}) async-start(f32[128,8,256]{2,1,0:T(8,128)} %broadcast_in_dim.12), calls=%async_computation.1 | async-start | bytes 2097152 | tf_op jit(solution)/shard_map/all_to_all | solution.py:174
  73.4 46.0 %copy-start.1 = (f32[256,256]{1,0:T(8,128)}, f32[256,256]{1,0:T(8,128)S(1)}, u32[]{:S(2)}) copy-start(f32[256,256]{1,0:T(8,128)S(1)} %get-tuple-element.27.a_ref) | copy-start | bytes 786436
  82.6 18.9 %all-to-all-start.2 = ((f32[8,128,256]{2,1,0:T(8,128)}), f32[8,128,256]{2,1,0:T(8,128)S(1)}, u32[]{:S(2)}, u32[]{:S(2)}) async-start(f32[8,128,256]{2,1,0:T(8,128)} %broadcast_in_dim.14), calls=%async_computation.2 | async-start | bytes 2097152 | tf_op jit(solution)/shard_map/all_to_all | solution.py:174
  102.4 15.2 %collective-permute-start.9 = (f32[256,256]{1,0:T(8,128)S(1)}, f32[256,256]{1,0:T(8,128)S(1)}, u32[]{:S(2)}, u32[]{:S(2)}) collective-permute-start(f32[256,256]{1,0:T(8,128)S(1)} %fusion.7), channel_id=1, source_target_pairs={{0,24},{2,26},{4,28},{6,30},{8,0},{10,2},{12,4},{14,6},{16,8},{18,... | collective-permute-start | bytes 786440 | tf_op jit(solution)/shard_map/ppermute | solution.py:190
  102.8 14.9 %collective-permute-start.8 = (f32[256,256]{1,0:T(8,128)S(1)}, f32[256,256]{1,0:T(8,128)S(1)}, u32[]{:S(2)}, u32[]{:S(2)}) collective-permute-start(f32[256,256]{1,0:T(8,128)S(1)} %fusion.7), channel_id=1, source_target_pairs={{0,8},{2,10},{4,12},{6,14},{8,16},{10,18},{12,20},{14,22},{16,24},... | collective-permute-start | bytes 786440 | tf_op jit(solution)/shard_map/ppermute | solution.py:190
  103.9 13.7 %collective-permute-start.7 = (f32[256,256]{1,0:T(8,128)S(1)}, f32[256,256]{1,0:T(8,128)S(1)}, u32[]{:S(2)}, u32[]{:S(2)}) collective-permute-start(f32[256,256]{1,0:T(8,128)S(1)} %fusion.7), channel_id=1, source_target_pairs={{0,16},{2,18},{4,20},{6,22},{8,24},{10,26},{12,28},{14,30},{16,0},... | collective-permute-start | bytes 786440 | tf_op jit(solution)/shard_map/ppermute | solution.py:190
  105.4 12.2 %all-to-all-start.3 = ((f32[16,1,256]{2,1,0:T(1,128)}), f32[16,1,256]{2,1,0:T(1,128)S(1)}, u32[]{:S(2)}, u32[]{:S(2)}) async-start(f32[16,1,256]{2,1,0:T(1,128)} %broadcast_in_dim.15), calls=%async_computation.3 | async-start | bytes 32768 | tf_op jit(solution)/shard_map/all_to_all | solution.py:174
  117.7 9.5 %collective-permute-start.12 = (f32[256,256]{1,0:T(8,128)S(1)}, f32[256,256]{1,0:T(8,128)S(1)}, u32[]{:S(2)}, u32[]{:S(2)}) collective-permute-start(f32[256,256]{1,0:T(8,128)S(1)} %add_add_fusion.1), channel_id=1, source_target_pairs={{0,6},{2,0},{4,2},{6,4},{8,14},{10,8},{12,10},{14,12},{16,22},{18,... | collective-permute-start | bytes 786440 | tf_op jit(solution)/shard_map/ppermute | solution.py:190
  118.1 9.2 %collective-permute-start.11 = (f32[256,256]{1,0:T(8,128)S(1)}, f32[256,256]{1,0:T(8,128)S(1)}, u32[]{:S(2)}, u32[]{:S(2)}) collective-permute-start(f32[256,256]{1,0:T(8,128)S(1)} %add_add_fusion.1), channel_id=1, source_target_pairs={{0,2},{2,4},{4,6},{6,0},{8,10},{10,12},{12,14},{14,8},{16,18},{18,... | collective-permute-start | bytes 786440 | tf_op jit(solution)/shard_map/ppermute | solution.py:190
  119.2 10.5 %collective-permute-start.10 = (f32[256,256]{1,0:T(8,128)S(1)}, f32[256,256]{1,0:T(8,128)S(1)}, u32[]{:S(2)}, u32[]{:S(2)}) collective-permute-start(f32[256,256]{1,0:T(8,128)S(1)} %add_add_fusion.1), channel_id=1, source_target_pairs={{0,4},{2,6},{4,0},{6,2},{8,12},{10,14},{12,8},{14,10},{16,20},{18,... | collective-permute-start | bytes 786440 | tf_op jit(solution)/shard_map/ppermute | solution.py:190
  119.4 25.7 %copy-start.2 = (f32[128,256]{1,0:T(8,128)}, f32[128,256]{1,0:T(8,128)S(1)}, u32[]{:S(2)}) copy-start(f32[128,256]{1,0:T(8,128)S(1)} %broadcast_divide_fusion.2.b_ref) | copy-start | bytes 393220
  130.5 17.4 %all-to-all-start.4 = ((f32[64,4,256]{2,1,0:T(4,128)}), f32[64,4,256]{2,1,0:T(4,128)S(1)}, u32[]{:S(2)}, u32[]{:S(2)}) async-start(f32[64,4,256]{2,1,0:T(4,128)} %reshape.46), calls=%async_computation.4 | async-start | bytes 524288 | tf_op jit(solution)/shard_map/all_to_all | solution.py:168
  148.9 19.1 %all-to-all-start.5 = ((f32[128,4,256]{2,1,0:T(4,128)}), f32[128,4,256]{2,1,0:T(4,128)S(1)}, u32[]{:S(2)}, u32[]{:S(2)}) async-start(f32[128,4,256]{2,1,0:T(4,128)} %broadcast_in_dim.16), calls=%async_computation.5 | async-start | bytes 1048576 | tf_op jit(solution)/shard_map/all_to_all | solution.py:174
where the time goes:
time: 170 us
  Pallas kernels  63.2 us (37%)
  starting transfers between devices  49.4 us (29%)
  waiting for transfers between devices  43.9 us (26%)
  matrix products  6.17 us (4%)
  local copies, waits for them, and re-layouts  4.82 us (3%)
    pallas_call x4, Pallas kernels, inverse_of(): pl.pallas_call(functools.partial(inverse_kernel, first, last), out_shape=...  38.4 us
    all_to_all x4, waiting for transfers between devices, gather_rows(): lax.all_to_all(copies, axes, 0, 0).reshape(n * x.shape[0], x.shape[1])  25.4 us
    pallas_call x3, Pallas kernels, tensor_pass(): pl.pallas_call(kernel, out_shape=jax.ShapeDtypeStruct((rows, rank), jnp.f...  24.8 us
    all_to_all x4, starting transfers between devices, gather_rows(): lax.all_to_all(copies, axes, 0, 0).reshape(n * x.shape[0], x.shape[1])  19.2 us
    ppermute x12, starting transfers between devices, sum_along(): parts.append(lax.ppermute(x, 'ja', pairs))  14.4 us
    all_to_all x2, waiting for transfers between devices, scatter_sum(): return jnp.sum(lax.all_to_all(pieces, axes, 0, 0), axis=0)  13.8 us
    all_to_all x2, starting transfers between devices, scatter_sum(): return jnp.sum(lax.all_to_all(pieces, axes, 0, 0), axis=0)  13 us
    ppermute x12, waiting for transfers between devices, sum_along(): parts.append(lax.ppermute(x, 'ja', pairs))  4.73 us
  transfers between devices with their start and end apart: 19, of which 9 were waited for; matrix products, arithmetic and copies ran while one was open for 0% of the time, Pallas kernels for 32%

commit v1 on v0

--- a/solution.py
+++ b/solution.py
@@ -25,7 +25,6 @@
 
 def reciprocal(x):
     r = pl.reciprocal(x, approx=True)
-    r = r * (2.0 - x * r)
     return r * (2.0 - x * r)
 
 
@@ -296,7 +295,7 @@
     rows_i, cols_j, deep_k = tensor.shape
     rank = factor_b.shape[1]
     n_i, n_j, n_k = (lax.axis_size(axis) for axis in ("ia", "ja", "ka"))
-    me_i, me_k = lax.axis_index("ia"), lax.axis_index("ka")
+    me_k = lax.axis_index("ka")
     total_i, total_j, total_k = rows_i * n_i, cols_j * n_j, deep_k * n_k
     every = ("ia", "ja", "ka")
 
@@ -307,15 +306,15 @@
     gram_b = sum_along(gram_b, 1)
     gram_c = add_partner(gram_of(late_c), "ka", 1)
     shared_a = scatter_sum(partial_a, ("ja", "ka"))
-    gram_b, gram_c, shared_a = lax.optimization_barrier((gram_b, gram_c, shared_a))
-    moment_a = gather_rows(shared_a, every)
-    all_a = product(moment_a, inverse_of(gram_b, gram_c))
-    raw_gram_a = gram_of(all_a)
+    moment_a = gather_rows(shared_a, ("ja", "ka"))
+    raw_a = product(moment_a, inverse_of(gram_b, gram_c))
+    raw_gram_a = add_partner(gram_of(raw_a), "ia", 1)
+
+    partial_b = tensor_pass(second_kernel, cols_j, tensor, raw_a, factor_c, "second")
+    raw_gram_a, partial_b = lax.optimization_barrier((raw_gram_a, partial_b))
+    raw_gram_a = add_partner(raw_gram_a, "ia", 2)
     scale_a = jnp.sqrt(diagonal_of(raw_gram_a) / total_i + eps)
-    raw_a = lax.dynamic_slice_in_dim(all_a, me_i * rows_i, rows_i, 0)
     factor_a = raw_a / scale_a
-
-    partial_b = tensor_pass(second_kernel, cols_j, tensor, raw_a, factor_c, "second")
     moment_b = jnp.sum(gather_rows(partial_b, ("ia", "ka")).reshape(-1, cols_j, rank), axis=0)
     raw_b = product(moment_b, inverse_of(raw_gram_a, gram_c)) * scale_a
     sums_b = jnp.sum(gather_rows(jnp.sum(raw_b * raw_b, axis=0, keepdims=True), "ja"), axis=0)

time: 170 us -> 167 us (0.982)
  waiting for transfers between devices: 43.9 us -> 23.3 us
  blocking collectives: 0 us -> 14.6 us
  starting transfers between devices: 49.4 us -> 55.7 us
  matrix products: 6.17 us -> 4.3 us
    all_to_all x0 -> x1, blocking collectives: none -> 14.6 us  [scatter_sum(): return jnp.sum(lax.all_to_all(pieces, axes, 0, 0), axis=0)]
    all_to_all x2 -> x1, waiting for transfers between devices: 13.8 us -> 3.08 us  [scatter_sum(): return jnp.sum(lax.all_to_all(pieces, axes, 0, 0), axis=0)]
    all_to_all x4, waiting for transfers between devices: 25.4 us -> 16.6 us  [gather_rows(): lax.all_to_all(copies, axes, 0, 0).reshape(n * x.shape[0], x.shape[1])]
    ppermute x12, starting transfers between devices: 14.4 us -> 21.4 us  [sum_along(): parts.append(lax.ppermute(x, 'ja', pairs))]
    all_to_all x2 -> x1, starting transfers between devices: 13 us -> 6.8 us  [scatter_sum(): return jnp.sum(lax.all_to_all(pieces, axes, 0, 0), axis=0)]
    all_to_all x4, starting transfers between devices: 19.2 us -> 22.4 us  [gather_rows(): lax.all_to_all(copies, axes, 0, 0).reshape(n * x.shape[0], x.shape[1])]
    ppermute x1 -> x3, starting transfers between devices: 2.82 us -> 5.19 us  [add_partner(): return x + lax.ppermute(x, axis, [(i, i ^ step) for i in range(n)])]
  transfers between devices with their start and end apart: 19 -> 20, of which waited for: 9 -> 7; matrix products, arithmetic and copies ran while one was open for 0% -> 2% of each run, Pallas kernels for 32% -> 37%
where the time goes in v1:
time: 167 us
  Pallas kernels  61.7 us (37%)
  starting transfers between devices  55.7 us (33%)
  waiting for transfers between devices  23.3 us (14%)
  blocking collectives  14.6 us (9%)
  local copies, waits for them, and re-layouts  4.51 us (3%)
  matrix products  4.3 us (3%)
    pallas_call x4, Pallas kernels, inverse_of(): pl.pallas_call(functools.partial(inverse_kernel, first, last), out_shape=...  37.1 us
    pallas_call x3, Pallas kernels, tensor_pass(): pl.pallas_call(kernel, out_shape=jax.ShapeDtypeStruct((rows, rank), jnp.f...  24.7 us
    all_to_all x4, starting transfers between devices, gather_rows(): lax.all_to_all(copies, axes, 0, 0).reshape(n * x.shape[0], x.shape[1])  22.4 us
    ppermute x12, starting transfers between devices, sum_along(): parts.append(lax.ppermute(x, 'ja', pairs))  21.4 us
    all_to_all x4, waiting for transfers between devices, gather_rows(): lax.all_to_all(copies, axes, 0, 0).reshape(n * x.shape[0], x.shape[1])  16.6 us
    all_to_all x1, blocking collectives, scatter_sum(): return jnp.sum(lax.all_to_all(pieces, axes, 0, 0), axis=0)  14.6 us
    all_to_all x1, starting transfers between devices, scatter_sum(): return jnp.sum(lax.all_to_all(pieces, axes, 0, 0), axis=0)  6.8 us
    ppermute x3, starting transfers between devices, add_partner(): return x + lax.ppermute(x, axis, [(i, i ^ step) for i in range(n)])  5.19 us
  transfers between devices with their start and end apart: 20, of which 7 were waited for; matrix products, arithmetic and copies ran while one was open for 2% of the time, Pallas kernels for 37%

profile of v1, /device:TPU:1, one launch (start us, length us, event | category | flops | bytes accessed | tf_op | source)
XLA Modules:
  0.0 166.6 jit_solution(4334975693735038761)
XLA Ops:
  0.6 1.4 fusion.5
  2.1 4.5 %collective-permute-start = (f32[256,256]{1,0:T(8,128)S(1)}, f32[256,256]{1,0:T(8,128)S(1)}, u32[]{:S(2)}, u32[]{:S(2)}) collective-permute-start(f32[256,256]{1,0:T(8,128)S(1)} %fusion.5), channel_id=1, source_target_pairs={{0,16},{2,18},{4,20},{6,22},{8,24},{10,26},{12,28},{14,30},{16,0},... | collective-permute-start | bytes 786440 | tf_op jit(solution)/shard_map/ppermute | solution.py:189
  7.3 1.9 %collective-permute-start.2 = (f32[256,256]{1,0:T(8,128)S(1)}, f32[256,256]{1,0:T(8,128)S(1)}, u32[]{:S(2)}, u32[]{:S(2)}) collective-permute-start(f32[256,256]{1,0:T(8,128)S(1)} %fusion.5), channel_id=1, source_target_pairs={{0,24},{2,26},{4,28},{6,30},{8,0},{10,2},{12,4},{14,6},{16,8},{18,... | collective-permute-start | bytes 786440 | tf_op jit(solution)/shard_map/ppermute | solution.py:189
  9.3 8.8 %first.1 = f32[256,256]{1,0:T(8,128)} custom-call(bf16[256,128,256]{2,1,0:T(8,128)(2,1)} %t_ref.5, f32[128,256]{1,0:T(8,128)} %b_ref.1, f32[256,256]{1,0:T(8,128)} %c_ref.3), custom_call_target="tpu_custom_call" | custom-call | flops 4294967296 | bytes 16777216 | tf_op jit(solution)/shard_map/first/pallas_call | solution.py:275
  19.6 2.8 %collective-permute-start.6 = (f32[256,256]{1,0:T(8,128)S(1)}, f32[256,256]{1,0:T(8,128)S(1)}, u32[]{:S(2)}, u32[]{:S(2)}) collective-permute-start(f32[256,256]{1,0:T(8,128)S(1)} %fusion.6), channel_id=1, source_target_pairs={{0,1},{1,0},{2,3},{3,2},{4,5},{5,4},{6,7},{7,6},{8,9},{9,8},{10,11... | collective-permute-start | bytes 786440 | tf_op jit(solution)/shard_map/ppermute | solution.py:178
  22.5 2.9 %collective-permute-start.3 = (f32[256,256]{1,0:T(8,128)S(1)}, f32[256,256]{1,0:T(8,128)S(1)}, u32[]{:S(2)}, u32[]{:S(2)}) collective-permute-start(f32[256,256]{1,0:T(8,128)S(1)} %add_add_fusion.3), channel_id=1, source_target_pairs={{0,4},{2,6},{4,0},{6,2},{8,12},{10,14},{12,8},{14,10},{16,20},{18,... | collective-permute-start | bytes 786440 | tf_op jit(solution)/shard_map/ppermute | solution.py:189
  25.8 2.3 %collective-permute-start.5 = (f32[256,256]{1,0:T(8,128)S(1)}, f32[256,256]{1,0:T(8,128)S(1)}, u32[]{:S(2)}, u32[]{:S(2)}) collective-permute-start(f32[256,256]{1,0:T(8,128)S(1)} %add_add_fusion.3), channel_id=1, source_target_pairs={{0,6},{2,0},{4,2},{6,4},{8,14},{10,8},{12,10},{14,12},{16,22},{18,... | collective-permute-start | bytes 786440 | tf_op jit(solution)/shard_map/ppermute | solution.py:189
  28.1 14.6 %all_to_all.30 = f32[32,8,256]{2,1,0:T(8,128)S(1)} all-to-all(f32[32,8,256]{2,1,0:T(8,128)} %bitcast.16), channel_id=1, replica_groups=mesh['ia'=4,'ja'=16,'ka'=2] {'ja','ka'}, dimensions={0} | all-to-all | bytes 524288 | tf_op jit(solution)/shard_map/all_to_all | solution.py:167
  43.4 5.9 %all-to-all-start.1 = ((f32[32,8,256]{2,1,0:T(8,128)}), f32[32,8,256]{2,1,0:T(8,128)S(1)}, u32[]{:S(2)}, u32[]{:S(2)}) async-start(f32[32,8,256]{2,1,0:T(8,128)} %broadcast_in_dim.12), calls=%async_computation.1 | async-start | bytes 524288 | tf_op jit(solution)/shard_map/all_to_all | solution.py:173
  49.4 12.3 %inverse.4 = f32[256,256]{1,0:T(8,128)S(1)} custom-call(f32[256,256]{1,0:T(8,128)S(1)} %add_add_fusion.2.one_ref, f32[256,256]{1,0:T(8,128)S(1)} %add.72.two_ref), custom_call_target="tpu_custom_call" | custom-call | flops 17179869184 | bytes 786432 | tf_op jit(solution)/shard_map/inverse/pallas_call | solution.py:151
  62.8 1.1 collective-permute-start.7
  63.9 8.1 %second.1 = f32[128,256]{1,0:T(8,128)S(1)} custom-call(bf16[256,128,256]{2,1,0:T(8,128)(2,1)} %t_ref.5, f32[256,256]{1,0:T(8,128)S(1)} %fusion.1.a_ref, f32[256,256]{1,0:T(8,128)S(1)} %copy-done), custom_call_target="tpu_custom_call" | custom-call | flops 4294967296 | bytes 16777216 | tf_op jit(solution)/shard_map/second/pallas_call | solution.py:275
  72.0 1.2 collective-permute-start.8
  73.2 1.1 broadcast_in_dim.14
  74.3 5.5 %all-to-all-start.2 = ((f32[8,128,256]{2,1,0:T(8,128)}), f32[8,128,256]{2,1,0:T(8,128)S(1)}, u32[]{:S(2)}, u32[]{:S(2)}) async-start(f32[8,128,256]{2,1,0:T(8,128)} %broadcast_in_dim.14), calls=%async_computation.2 | async-start | bytes 2097152 | tf_op jit(solution)/shard_map/all_to_all | solution.py:173
  80.1 12.3 %inverse.5 = f32[256,256]{1,0:T(8,128)S(1)} custom-call(f32[256,256]{1,0:T(8,128)S(1)} %get-tuple-element.26.one_ref, f32[256,256]{1,0:T(8,128)S(1)} %add.72.two_ref), custom_call_target="tpu_custom_call" | custom-call | flops 17179869184 | bytes 786432 | tf_op jit(solution)/shard_map/inverse/pallas_call | solution.py:151
  92.4 2.4 %all-to-all-done.2 = f32[8,128,256]{2,1,0:T(8,128)S(1)} async-done(((f32[8,128,256]{2,1,0:T(8,128)}), f32[8,128,256]{2,1,0:T(8,128)S(1)}, u32[]{:S(2)}, u32[]{:S(2)}) %all-to-all-start.2) | async-done | bytes 1048608 | tf_op jit(solution)/shard_map/all_to_all | solution.py:173
  95.6 1.2 collective-permute-start.10
  96.8 1.5 collective-permute-start.11
  98.3 1.4 collective-permute-start.9
  100.4 5.3 %all-to-all-start.3 = ((f32[16,1,256]{2,1,0:T(1,128)}), f32[16,1,256]{2,1,0:T(1,128)S(1)}, u32[]{:S(2)}, u32[]{:S(2)}) async-start(f32[16,1,256]{2,1,0:T(1,128)} %broadcast_in_dim.15), calls=%async_computation.3 | async-start | bytes 32768 | tf_op jit(solution)/shard_map/all_to_all | solution.py:173
  105.7 6.4 %all-to-all-done.3 = f32[16,1,256]{2,1,0:T(1,128)S(1)} async-done(((f32[16,1,256]{2,1,0:T(1,128)}), f32[16,1,256]{2,1,0:T(1,128)S(1)}, u32[]{:S(2)}, u32[]{:S(2)}) %all-to-all-start.3) | async-done | bytes 16416 | tf_op jit(solution)/shard_map/all_to_all | solution.py:173
  112.3 1.7 %collective-permute-start.12 = (f32[256,256]{1,0:T(8,128)S(1)}, f32[256,256]{1,0:T(8,128)S(1)}, u32[]{:S(2)}, u32[]{:S(2)}) collective-permute-start(f32[256,256]{1,0:T(8,128)S(1)} %add_add_fusion.1), channel_id=1, source_target_pairs={{0,4},{2,6},{4,0},{6,2},{8,12},{10,14},{12,8},{14,10},{16,20},{18,... | collective-permute-start | bytes 786440 | tf_op jit(solution)/shard_map/ppermute | solution.py:189
  114.3 2.4 %collective-permute-start.14 = (f32[256,256]{1,0:T(8,128)S(1)}, f32[256,256]{1,0:T(8,128)S(1)}, u32[]{:S(2)}, u32[]{:S(2)}) collective-permute-start(f32[256,256]{1,0:T(8,128)S(1)} %add_add_fusion.1), channel_id=1, source_target_pairs={{0,6},{2,0},{4,2},{6,4},{8,14},{10,8},{12,10},{14,12},{16,22},{18,... | collective-permute-start | bytes 786440 | tf_op jit(solution)/shard_map/ppermute | solution.py:189
  116.7 7.8 %third.1 = f32[256,256]{1,0:T(8,128)S(1)} custom-call(bf16[256,128,256]{2,1,0:T(8,128)(2,1)} %t_ref.5, f32[256,256]{1,0:T(8,128)S(1)} %broadcast_divide_fusion.1.a_ref, f32[128,256]{1,0:T(8,128)S(1)} %broadcast_divide_fusion.2.b_ref), custom_call_target="tpu_custom_call" | custom-call | flops 4294967296 | bytes 16777216 | tf_op jit(solution)/shard_map/third/pallas_call | solution.py:275
  124.6 2.4 %collective-permute-done.13 = f32[256,256]{1,0:T(8,128)S(1)} collective-permute-done((f32[256,256]{1,0:T(8,128)S(1)}, f32[256,256]{1,0:T(8,128)S(1)}, u32[]{:S(2)}, u32[]{:S(2)}) %collective-permute-start.13) | collective-permute-done | bytes 262176 | tf_op jit(solution)/shard_map/ppermute | solution.py:189
  127.8 6.8 %all-to-all-start.4 = ((f32[64,4,256]{2,1,0:T(4,128)}), f32[64,4,256]{2,1,0:T(4,128)S(1)}, u32[]{:S(2)}, u32[]{:S(2)}) async-start(f32[64,4,256]{2,1,0:T(4,128)} %reshape.46), calls=%async_computation.4 | async-start | bytes 524288 | tf_op jit(solution)/shard_map/all_to_all | solution.py:167
  134.6 6.2 %inverse.6.rest_0_ = f32[256,256]{1,0:T(8,128)S(1)} custom-call(f32[256,256]{1,0:T(8,128)S(1)} %get-tuple-element.26.one_ref, f32[256,256]{1,0:T(8,128)S(1)} %add_add_fusion.two_ref), custom_call_target="tpu_custom_call" | custom-call | flops 8589934592 | bytes 786432 | tf_op jit(solution)/shard_map/inverse/pallas_call | solution.py:151
  140.9 3.1 %all-to-all-done.4 = f32[64,4,256]{2,1,0:T(4,128)S(1)} async-done(((f32[64,4,256]{2,1,0:T(4,128)}), f32[64,4,256]{2,1,0:T(4,128)S(1)}, u32[]{:S(2)}, u32[]{:S(2)}) %all-to-all-start.4) | async-done | bytes 262176 | tf_op jit(solution)/shard_map/all_to_all | solution.py:167
  144.9 5.7 %all-to-all-start.5 = ((f32[128,4,256]{2,1,0:T(4,128)}), f32[128,4,256]{2,1,0:T(4,128)S(1)}, u32[]{:S(2)}, u32[]{:S(2)}) async-start(f32[128,4,256]{2,1,0:T(4,128)} %broadcast_in_dim.16), calls=%async_computation.5 | async-start | bytes 1048576 | tf_op jit(solution)/shard_map/all_to_all | solution.py:173
  150.7 6.2 %inverse.7 = f32[256,256]{1,0:T(8,128)S(1)} custom-call(f32[256,256]{1,0:T(8,128)S(1)} %get-tuple-element.26.one_ref, f32[256,256]{1,0:T(8,128)S(1)} %add_add_fusion.two_ref, f32[256,256]{1,0:T(8,128)S(1)} %inverse.6.rest_0_), custom_call_target="tpu_custom_call" | custom-call | flops 8589934592 | bytes 786432 | tf_op jit(solution)/shard_map/inverse/pallas_call | solution.py:151
  156.9 7.9 %all-to-all-done.5 = f32[128,4,256]{2,1,0:T(4,128)S(1)} async-done(((f32[128,4,256]{2,1,0:T(4,128)}), f32[128,4,256]{2,1,0:T(4,128)S(1)}, u32[]{:S(2)}, u32[]{:S(2)}) %all-to-all-start.5) | async-done | bytes 524320 | tf_op jit(solution)/shard_map/all_to_all | solution.py:173
  (56 shorter events, 10.4 us)
Async XLA Ops:
  0.6 18.4 %copy-start = (f32[256,256]{1,0:T(8,128)S(1)}, f32[256,256]{1,0:T(8,128)}, u32[]{:S(2)}) copy-start(f32[256,256]{1,0:T(8,128)} %c_ref.3) | copy-start | bytes 786436
  2.1 16.0 %collective-permute-start = (f32[256,256]{1,0:T(8,128)S(1)}, f32[256,256]{1,0:T(8,128)S(1)}, u32[]{:S(2)}, u32[]{:S(2)}) collective-permute-start(f32[256,256]{1,0:T(8,128)S(1)} %fusion.5), channel_id=1, source_target_pairs={{0,16},{2,18},{4,20},{6,22},{8,24},{10,26},{12,28},{14,30},{16,0},... | collective-permute-start | bytes 786440 | tf_op jit(solution)/shard_map/ppermute | solution.py:189
  6.6 12.4 %collective-permute-start.1 = (f32[256,256]{1,0:T(8,128)S(1)}, f32[256,256]{1,0:T(8,128)S(1)}, u32[]{:S(2)}, u32[]{:S(2)}) collective-permute-start(f32[256,256]{1,0:T(8,128)S(1)} %fusion.5), channel_id=1, source_target_pairs={{0,8},{2,10},{4,12},{6,14},{8,16},{10,18},{12,20},{14,22},{16,24},... | collective-permute-start | bytes 786440 | tf_op jit(solution)/shard_map/ppermute | solution.py:189
  7.3 11.7 %collective-permute-start.2 = (f32[256,256]{1,0:T(8,128)S(1)}, f32[256,256]{1,0:T(8,128)S(1)}, u32[]{:S(2)}, u32[]{:S(2)}) collective-permute-start(f32[256,256]{1,0:T(8,128)S(1)} %fusion.5), channel_id=1, source_target_pairs={{0,24},{2,26},{4,28},{6,30},{8,0},{10,2},{12,4},{14,6},{16,8},{18,... | collective-permute-start | bytes 786440 | tf_op jit(solution)/shard_map/ppermute | solution.py:189
  19.6 29.6 %collective-permute-start.6 = (f32[256,256]{1,0:T(8,128)S(1)}, f32[256,256]{1,0:T(8,128)S(1)}, u32[]{:S(2)}, u32[]{:S(2)}) collective-permute-start(f32[256,256]{1,0:T(8,128)S(1)} %fusion.6), channel_id=1, source_target_pairs={{0,1},{1,0},{2,3},{3,2},{4,5},{5,4},{6,7},{7,6},{8,9},{9,8},{10,11... | collective-permute-start | bytes 786440 | tf_op jit(solution)/shard_map/ppermute | solution.py:178
  22.5 26.9 %collective-permute-start.3 = (f32[256,256]{1,0:T(8,128)S(1)}, f32[256,256]{1,0:T(8,128)S(1)}, u32[]{:S(2)}, u32[]{:S(2)}) collective-permute-start(f32[256,256]{1,0:T(8,128)S(1)} %add_add_fusion.3), channel_id=1, source_target_pairs={{0,4},{2,6},{4,0},{6,2},{8,12},{10,14},{12,8},{14,10},{16,20},{18,... | collective-permute-start | bytes 786440 | tf_op jit(solution)/shard_map/ppermute | solution.py:189
  25.4 24.0 %collective-permute-start.4 = (f32[256,256]{1,0:T(8,128)S(1)}, f32[256,256]{1,0:T(8,128)S(1)}, u32[]{:S(2)}, u32[]{:S(2)}) collective-permute-start(f32[256,256]{1,0:T(8,128)S(1)} %add_add_fusion.3), channel_id=1, source_target_pairs={{0,2},{2,4},{4,6},{6,0},{8,10},{10,12},{12,14},{14,8},{16,18},{18,... | collective-permute-start | bytes 786440 | tf_op jit(solution)/shard_map/ppermute | solution.py:189
  25.8 23.6 %collective-permute-start.5 = (f32[256,256]{1,0:T(8,128)S(1)}, f32[256,256]{1,0:T(8,128)S(1)}, u32[]{:S(2)}, u32[]{:S(2)}) collective-permute-start(f32[256,256]{1,0:T(8,128)S(1)} %add_add_fusion.3), channel_id=1, source_target_pairs={{0,6},{2,0},{4,2},{6,4},{8,14},{10,8},{12,10},{14,12},{16,22},{18,... | collective-permute-start | bytes 786440 | tf_op jit(solution)/shard_map/ppermute | solution.py:189
  43.4 18.4 %all-to-all-start.1 = ((f32[32,8,256]{2,1,0:T(8,128)}), f32[32,8,256]{2,1,0:T(8,128)S(1)}, u32[]{:S(2)}, u32[]{:S(2)}) async-start(f32[32,8,256]{2,1,0:T(8,128)} %broadcast_in_dim.12), calls=%async_computation.1 | async-start | bytes 524288 | tf_op jit(solution)/shard_map/all_to_all | solution.py:173
  62.8 9.2 %collective-permute-start.7 = (f32[256,256]{1,0:T(8,128)S(1)}, f32[256,256]{1,0:T(8,128)S(1)}, u32[]{:S(2)}, u32[]{:S(2)}) collective-permute-start(f32[256,256]{1,0:T(8,128)S(1)} %fusion.7), channel_id=1, source_target_pairs={{0,32},{32,0},{64,96},{96,64},{1,33},{33,1},{65,97},{97,65},{2,34}... | collective-permute-start | bytes 786440 | tf_op jit(solution)/shard_map/ppermute | solution.py:178
  72.0 8.0 %collective-permute-start.8 = (f32[256,256]{1,0:T(8,128)S(1)}, f32[256,256]{1,0:T(8,128)S(1)}, u32[]{:S(2)}, u32[]{:S(2)}) collective-permute-start(f32[256,256]{1,0:T(8,128)S(1)} %add.73), channel_id=1, source_target_pairs={{0,64},{32,96},{64,0},{96,32},{1,65},{33,97},{65,1},{97,33},{2,66}... | collective-permute-start | bytes 786440 | tf_op jit(solution)/shard_map/ppermute | solution.py:178
  74.3 20.5 %all-to-all-start.2 = ((f32[8,128,256]{2,1,0:T(8,128)}), f32[8,128,256]{2,1,0:T(8,128)S(1)}, u32[]{:S(2)}, u32[]{:S(2)}) async-start(f32[8,128,256]{2,1,0:T(8,128)} %broadcast_in_dim.14), calls=%async_computation.2 | async-start | bytes 2097152 | tf_op jit(solution)/shard_map/all_to_all | solution.py:173
  95.6 16.6 %collective-permute-start.10 = (f32[256,256]{1,0:T(8,128)S(1)}, f32[256,256]{1,0:T(8,128)S(1)}, u32[]{:S(2)}, u32[]{:S(2)}) collective-permute-start(f32[256,256]{1,0:T(8,128)S(1)} %fusion.8), channel_id=1, source_target_pairs={{0,8},{2,10},{4,12},{6,14},{8,16},{10,18},{12,20},{14,22},{16,24},... | collective-permute-start | bytes 786440 | tf_op jit(solution)/shard_map/ppermute | solution.py:189
  96.8 15.4 %collective-permute-start.11 = (f32[256,256]{1,0:T(8,128)S(1)}, f32[256,256]{1,0:T(8,128)S(1)}, u32[]{:S(2)}, u32[]{:S(2)}) collective-permute-start(f32[256,256]{1,0:T(8,128)S(1)} %fusion.8), channel_id=1, source_target_pairs={{0,24},{2,26},{4,28},{6,30},{8,0},{10,2},{12,4},{14,6},{16,8},{18,... | collective-permute-start | bytes 786440 | tf_op jit(solution)/shard_map/ppermute | solution.py:189
  98.3 13.9 %collective-permute-start.9 = (f32[256,256]{1,0:T(8,128)S(1)}, f32[256,256]{1,0:T(8,128)S(1)}, u32[]{:S(2)}, u32[]{:S(2)}) collective-permute-start(f32[256,256]{1,0:T(8,128)S(1)} %fusion.8), channel_id=1, source_target_pairs={{0,16},{2,18},{4,20},{6,22},{8,24},{10,26},{12,28},{14,30},{16,0},... | collective-permute-start | bytes 786440 | tf_op jit(solution)/shard_map/ppermute | solution.py:189
  100.4 11.8 %all-to-all-start.3 = ((f32[16,1,256]{2,1,0:T(1,128)}), f32[16,1,256]{2,1,0:T(1,128)S(1)}, u32[]{:S(2)}, u32[]{:S(2)}) async-start(f32[16,1,256]{2,1,0:T(1,128)} %broadcast_in_dim.15), calls=%async_computation.3 | async-start | bytes 32768 | tf_op jit(solution)/shard_map/all_to_all | solution.py:173
  105.7 35.1 %copy-start.1 = (f32[256,256]{1,0:T(8,128)}, f32[256,256]{1,0:T(8,128)S(1)}, u32[]{:S(2)}) copy-start(f32[256,256]{1,0:T(8,128)S(1)} %broadcast_divide_fusion.1.a_ref) | copy-start | bytes 786436
  112.3 12.3 %collective-permute-start.12 = (f32[256,256]{1,0:T(8,128)S(1)}, f32[256,256]{1,0:T(8,128)S(1)}, u32[]{:S(2)}, u32[]{:S(2)}) collective-permute-start(f32[256,256]{1,0:T(8,128)S(1)} %add_add_fusion.1), channel_id=1, source_target_pairs={{0,4},{2,6},{4,0},{6,2},{8,12},{10,14},{12,8},{14,10},{16,20},{18,... | collective-permute-start | bytes 786440 | tf_op jit(solution)/shard_map/ppermute | solution.py:189
  114.0 13.0 %collective-permute-start.13 = (f32[256,256]{1,0:T(8,128)S(1)}, f32[256,256]{1,0:T(8,128)S(1)}, u32[]{:S(2)}, u32[]{:S(2)}) collective-permute-start(f32[256,256]{1,0:T(8,128)S(1)} %add_add_fusion.1), channel_id=1, source_target_pairs={{0,2},{2,4},{4,6},{6,0},{8,10},{10,12},{12,14},{14,8},{16,18},{18,... | collective-permute-start | bytes 786440 | tf_op jit(solution)/shard_map/ppermute | solution.py:189
  114.3 12.7 %collective-permute-start.14 = (f32[256,256]{1,0:T(8,128)S(1)}, f32[256,256]{1,0:T(8,128)S(1)}, u32[]{:S(2)}, u32[]{:S(2)}) collective-permute-start(f32[256,256]{1,0:T(8,128)S(1)} %add_add_fusion.1), channel_id=1, source_target_pairs={{0,6},{2,0},{4,2},{6,4},{8,14},{10,8},{12,10},{14,12},{16,22},{18,... | collective-permute-start | bytes 786440 | tf_op jit(solution)/shard_map/ppermute | solution.py:189
  116.7 24.2 %copy-start.2 = (f32[128,256]{1,0:T(8,128)}, f32[128,256]{1,0:T(8,128)S(1)}, u32[]{:S(2)}) copy-start(f32[128,256]{1,0:T(8,128)S(1)} %broadcast_divide_fusion.2.b_ref) | copy-start | bytes 393220
  127.8 16.1 %all-to-all-start.4 = ((f32[64,4,256]{2,1,0:T(4,128)}), f32[64,4,256]{2,1,0:T(4,128)S(1)}, u32[]{:S(2)}, u32[]{:S(2)}) async-start(f32[64,4,256]{2,1,0:T(4,128)} %reshape.46), calls=%async_computation.4 | async-start | bytes 524288 | tf_op jit(solution)/shard_map/all_to_all | solution.py:167
  144.9 19.8 %all-to-all-start.5 = ((f32[128,4,256]{2,1,0:T(4,128)}), f32[128,4,256]{2,1,0:T(4,128)S(1)}, u32[]{:S(2)}, u32[]{:S(2)}) async-start(f32[128,4,256]{2,1,0:T(4,128)} %broadcast_in_dim.16), calls=%async_computation.5 | async-start | bytes 1048576 | tf_op jit(solution)/shard_map/all_to_all | solution.py:173

commit v2 on v1

--- a/solution.py
+++ b/solution.py
@@ -55,74 +55,99 @@
     return terms[0]
 
 
-def eliminate(w, first, last):
+def eliminate_panel(x):
+    tiles, groups = len(x[0]), len(x)
+    sub = lax.broadcasted_iota(jnp.int32, (8, 128), 0)
+    lane = lax.broadcasted_iota(jnp.int32, (8, 128), 1)
+    for q in range(groups):
+        l = 8 * q
+        inside = (lane >= l) & (lane < l + 8)
+        columns = [
+            [jnp.broadcast_to(x[g][0][:, l + j : l + j + 1], (8, 128)) for j in range(8)]
+            for g in range(groups)
+        ]
+        a = [
+            [jnp.broadcast_to(columns[q][j][i : i + 1, :], (8, 128)) for j in range(i + 1)]
+            for i in range(8)
+        ]
+        a = sweep(a, 8)
+        inverse = []
+        for j in range(8):
+            column = a[7][j]
+            for i in range(7):
+                column = jnp.where(sub == i, a[max(i, j)][min(i, j)], column)
+            inverse.append(column)
+        source = list(x[q])
+        source[0] = jnp.where(inside, (lane - l == sub).astype(jnp.float32), source[0])
+        x[q] = [
+            -total_of(
+                [
+                    inverse[j] * jnp.broadcast_to(source[h][j : j + 1, :], (8, 128))
+                    for j in range(8)
+                ]
+            )
+            for h in range(tiles)
+        ]
+        rows = [
+            [jnp.broadcast_to(x[q][h][j : j + 1, :], (8, 128)) for j in range(8)]
+            for h in range(tiles)
+        ]
+        for g in range(groups):
+            if g == q:
+                continue
+            for h in range(tiles):
+                base = jnp.where(inside, 0.0, x[g][h]) if h == 0 else x[g][h]
+                x[g][h] = base - total_of([columns[g][j] * rows[h][j] for j in range(8)])
+    return x
+
+
+def minus_update(rows, across, panel):
+    place = lax.broadcasted_iota(jnp.int32, rows.shape, 1)
+    return jnp.where(place < PANEL, 0.0, rows) - lax.dot_general(
+        across,
+        panel,
+        (((0,), (0,)), ((), ())),
+        precision=lax.Precision.HIGHEST,
+        preferred_element_type=jnp.float32,
+    )
+
+
+def eliminate(w, next_ref, across_ref, panel_ref, first, last):
     n = w.shape[0]
     tiles, groups = n // 128, PANEL // 8
-    sub = lax.broadcasted_iota(jnp.int32, (8, 128), 0)
-    lane = lax.broadcasted_iota(jnp.int32, (8, 128), 1)
+
+    def panel_of(p):
+        x = [
+            [next_ref[8 * g : 8 * g + 8, 128 * h : 128 * h + 128] for h in range(tiles)]
+            for g in range(groups)
+        ]
+        x = eliminate_panel(x)
+        place = lax.broadcasted_iota(jnp.int32, (PANEL, n), 1)
+        across = jnp.where(place >= n - PANEL * p, -next_ref[...], next_ref[...])
+        rows = [jnp.concatenate(x[g], axis=1) for g in range(groups)]
+        return across, jnp.concatenate(rows, axis=0)
+
+    def follow(across, panel):
+        rows = minus_update(w[PANEL : 2 * PANEL, :], across[:, PANEL : 2 * PANEL], panel)
+        next_ref[...] = pltpu.roll(rows, n - PANEL, 1)
+        across_ref[...] = across
+        panel_ref[...] = panel
+
+    def catch_up():
+        rest = minus_update(w[PANEL:, :], across_ref[:, PANEL:], panel_ref[...])
+        w[0 : n - PANEL, :] = pltpu.roll(rest, n - PANEL, 1)
+        w[n - PANEL :, :] = pltpu.roll(panel_ref[...], n - PANEL, 1)
 
     def step(p, carry):
-        x = [
-            [w[8 * g : 8 * g + 8, 128 * h : 128 * h + 128] for h in range(tiles)]
-            for g in range(groups)
-        ]
-        old = w[0:PANEL, :]
-        for q in range(groups):
-            l = 8 * q
-            inside = (lane >= l) & (lane < l + 8)
-            columns = [
-                [jnp.broadcast_to(x[g][0][:, l + j : l + j + 1], (8, 128)) for j in range(8)]
-                for g in range(groups)
-            ]
-            a = [
-                [jnp.broadcast_to(columns[q][j][i : i + 1, :], (8, 128)) for j in range(i + 1)]
-                for i in range(8)
-            ]
-            a = sweep(a, 8)
-            inverse = []
-            for j in range(8):
-                column = a[7][j]
-                for i in range(7):
-                    column = jnp.where(sub == i, a[max(i, j)][min(i, j)], column)
-                inverse.append(column)
-            source = list(x[q])
-            source[0] = jnp.where(inside, (lane - l == sub).astype(jnp.float32), source[0])
-            x[q] = [
-                -total_of(
-                    [
-                        inverse[j] * jnp.broadcast_to(source[h][j : j + 1, :], (8, 128))
-                        for j in range(8)
-                    ]
-                )
-                for h in range(tiles)
-            ]
-            rows = [
-                [jnp.broadcast_to(x[q][h][j : j + 1, :], (8, 128)) for j in range(8)]
-                for h in range(tiles)
-            ]
-            for g in range(groups):
-                if g == q:
-                    continue
-                for h in range(tiles):
-                    base = jnp.where(inside, 0.0, x[g][h]) if h == 0 else x[g][h]
-                    x[g][h] = base - total_of([columns[g][j] * rows[h][j] for j in range(8)])
-        panel = jnp.concatenate([jnp.concatenate(x[g], axis=1) for g in range(groups)], axis=0)
-        place = lax.broadcasted_iota(jnp.int32, (PANEL, n), 1)
-        across = jnp.where(place >= n - PANEL * p, -old, old)
-        update = lax.dot_general(
-            across,
-            panel,
-            (((0,), (0,)), ((), ())),
-            precision=lax.Precision.HIGHEST,
-            preferred_element_type=jnp.float32,
-        )
-        place = lax.broadcasted_iota(jnp.int32, (n - PANEL, n), 1)
-        rest = jnp.where(place < PANEL, 0.0, w[PANEL:, :]) - update[PANEL:, :]
-        w[0 : n - PANEL, :] = pltpu.roll(rest, n - PANEL, 1)
-        w[n - PANEL :, :] = pltpu.roll(panel, n - PANEL, 1)
+        across, panel = panel_of(p)
+        catch_up()
+        follow(across, panel)
         return carry
 
-    lax.fori_loop(first, last, step, 0)
+    next_ref[...] = w[0:PANEL, :]
+    follow(*panel_of(first))
+    lax.fori_loop(first + 1, last, step, 0)
+    catch_up()
 
 
 def mixed_of(one_ref, two_ref):
@@ -136,10 +161,10 @@
 
 
 def inverse_kernel(first, last, one_ref, two_ref, *rest):
-    out_ref = rest[-1]
+    out_ref, held = rest[-4], rest[-3:]
     mixed, down, along = mixed_of(one_ref, two_ref)
     out_ref[...] = mixed * down * along if first == 0 else rest[0][...]
-    eliminate(out_ref, first, last)
+    eliminate(out_ref, *held, first, last)
     if last == out_ref.shape[0] // PANEL:
         out_ref[...] = out_ref[...] * down * along
 
@@ -153,6 +178,7 @@
         out_shape=jax.ShapeDtypeStruct((n, n), jnp.float32),
         in_specs=[whole] * (2 + len(state)),
         out_specs=whole,
+        scratch_shapes=[pltpu.VMEM((PANEL, n), jnp.float32)] * 3,
         compiler_params=pltpu.CompilerParams(vmem_limit_bytes=6 << 20),
         cost_estimate=pl.CostEstimate(
             flops=(last - first) << 31, bytes_accessed=12 * n * n, transcendentals=0
@@ -246,27 +272,33 @@
 
 def second_kernel(t_ref, a_ref, c_ref, out_ref, held_ref, sems):
     def use(part, flat):
-        out_ref[...] += jnp.sum(inner_of(flat, c_ref) * a_ref[part, :][:, None, :], axis=0)
-
-    out_ref[...] = jnp.zeros_like(out_ref)
+        out_ref[0] += jnp.sum(inner_of(flat, c_ref) * a_ref[part, :][:, None, :], axis=0)
+
+    out_ref[0] = jnp.zeros_like(out_ref[0])
     over_chunks(t_ref, held_ref, sems, use)
-
-
-def third_kernel(t_ref, a_ref, b_ref, out_ref, held_ref, sems):
+    for copy in range(1, out_ref.shape[0]):
+        out_ref[copy] = out_ref[0]
+
+
+def third_kernel(t_ref, a_ref, b_ref, out_ref, held_ref, sems, sum_ref):
     def use(part, flat):
         paired = (a_ref[part, :][:, None, :] * b_ref[...][None]).astype(jnp.bfloat16)
-        out_ref[...] += lax.dot_general(
+        sum_ref[...] += lax.dot_general(
             flat,
             paired.reshape(flat.shape[0], b_ref.shape[1]),
             (((0,), (0,)), ((), ())),
             preferred_element_type=jnp.float32,
         )
 
-    out_ref[...] = jnp.zeros_like(out_ref)
+    sum_ref[...] = jnp.zeros_like(sum_ref)
     over_chunks(t_ref, held_ref, sems, use)
-
-
-def tensor_pass(kernel, rows, tensor, one, two, name):
+    across = sum_ref.shape[1] // 128
+    for piece in range(out_ref.shape[0]):
+        t, h = divmod(piece, across)
+        out_ref[piece] = sum_ref[8 * t : 8 * t + 8, 128 * h : 128 * h + 128]
+
+
+def tensor_pass(kernel, shape, tensor, one, two, name, scratch=()):
     rank = one.shape[1]
     whole = pl.BlockSpec(memory_space=pltpu.VMEM)
     away = pl.BlockSpec(memory_space=pl.ANY)
@@ -274,7 +306,7 @@
     small = [pltpu.VMEM(x.shape, x.dtype) for x in (one, two)] if fetched else []
     return pl.pallas_call(
         kernel,
-        out_shape=jax.ShapeDtypeStruct((rows, rank), jnp.float32),
+        out_shape=jax.ShapeDtypeStruct(shape, jnp.float32),
         in_specs=[away] + [away if fetched else whole] * 2,
         out_specs=whole,
         scratch_shapes=[
@@ -282,6 +314,7 @@
             pltpu.SemaphoreType.DMA((tensor.shape[0] // CHUNK,)),
         ]
         + small
+        + list(scratch)
         + [pltpu.SemaphoreType.DMA] * len(small),
         compiler_params=pltpu.CompilerParams(vmem_limit_bytes=(60 if fetched else 48) << 20),
         cost_estimate=pl.CostEstimate(
@@ -295,27 +328,34 @@
     rows_i, cols_j, deep_k = tensor.shape
     rank = factor_b.shape[1]
     n_i, n_j, n_k = (lax.axis_size(axis) for axis in ("ia", "ja", "ka"))
-    me_k = lax.axis_index("ka")
+    me_i, me_k = lax.axis_index("ia"), lax.axis_index("ka")
     total_i, total_j, total_k = rows_i * n_i, cols_j * n_j, deep_k * n_k
     every = ("ia", "ja", "ka")
 
-
-    gram_b = sum_along(gram_of(factor_b), 0)
-    partial_a = tensor_pass(first_kernel, rows_i, tensor, factor_b, factor_c, "first")
-    gram_b, late_c, partial_a = lax.optimization_barrier((gram_b, factor_c, partial_a))
-    gram_b = sum_along(gram_b, 1)
+    half = rank // 2
+    core = me_i % 2
+    own = lax.dynamic_slice_in_dim(factor_b, core * half, half, 1)
+    part = sum_along(product(own.T, factor_b), 0)
+    partial_a = tensor_pass(first_kernel, (rows_i, rank), tensor, factor_b, factor_c, "first")
+    part, late_c, partial_a = lax.optimization_barrier((part, factor_c, partial_a))
+    part = sum_along(part, 1)
     gram_c = add_partner(gram_of(late_c), "ka", 1)
+    other = lax.ppermute(part, "ia", [(i, i ^ 1) for i in range(n_i)])
+    gram_b = jnp.concatenate(
+        [jnp.where(core == 0, part, other), jnp.where(core == 0, other, part)], axis=0
+    )
     shared_a = scatter_sum(partial_a, ("ja", "ka"))
     moment_a = gather_rows(shared_a, ("ja", "ka"))
     raw_a = product(moment_a, inverse_of(gram_b, gram_c))
     raw_gram_a = add_partner(gram_of(raw_a), "ia", 1)
 
-    partial_b = tensor_pass(second_kernel, cols_j, tensor, raw_a, factor_c, "second")
+    copies = (n_i * n_k, cols_j, rank)
+    partial_b = tensor_pass(second_kernel, copies, tensor, raw_a, factor_c, "second")
     raw_gram_a, partial_b = lax.optimization_barrier((raw_gram_a, partial_b))
     raw_gram_a = add_partner(raw_gram_a, "ia", 2)
     scale_a = jnp.sqrt(diagonal_of(raw_gram_a) / total_i + eps)
     factor_a = raw_a / scale_a
-    moment_b = jnp.sum(gather_rows(partial_b, ("ia", "ka")).reshape(-1, cols_j, rank), axis=0)
+    moment_b = jnp.sum(lax.all_to_all(partial_b, ("ia", "ka"), 0, 0), axis=0)
     raw_b = product(moment_b, inverse_of(raw_gram_a, gram_c)) * scale_a
     sums_b = jnp.sum(gather_rows(jnp.sum(raw_b * raw_b, axis=0, keepdims=True), "ja"), axis=0)
     scale_b = jnp.sqrt(sums_b / total_j + eps)
@@ -324,19 +364,28 @@
     raw_gram_b = sum_along(raw_gram_b, 1)
     refit_b = raw_b / scale_b
 
-    partial_c = tensor_pass(third_kernel, deep_k, tensor, factor_a, refit_b, "third")
+    down, across = deep_k // 8, rank // 128
+    partial_c = tensor_pass(
+        third_kernel,
+        (down * across, 8, 128),
+        tensor,
+        factor_a,
+        refit_b,
+        "third",
+        [pltpu.VMEM((deep_k, rank), jnp.float32)],
+    )
     raw_gram_b, partial_c = lax.optimization_barrier((raw_gram_b, partial_c))
-    shared_c = scatter_sum(partial_c, ("ia", "ja"))
-    half = rank // PANEL // 2
-    state = inverse_of(raw_gram_a, raw_gram_b, 0, half)
+    shared_c = scatter_sum(partial_c.reshape(-1, 128), ("ia", "ja"))
+    middle = rank // PANEL // 2
+    state = inverse_of(raw_gram_a, raw_gram_b, 0, middle)
     state, shared_c = lax.optimization_barrier((state, shared_c))
-    moment_c = gather_rows(shared_c, every)
-    inverse_c = inverse_of(raw_gram_a, raw_gram_b, half, None, (state,))
+    pieces = gather_rows(shared_c, every).reshape(down, across, n_k, 8, 128)
+    moment_c = pieces.transpose(2, 0, 3, 1, 4).reshape(total_k, rank)
+    inverse_c = inverse_of(raw_gram_a, raw_gram_b, middle, None, (state,))
     both = scale_a * scale_b
     all_c = product(moment_c * both, inverse_c) * both
     scale_c = jnp.sqrt(jnp.sum(all_c * all_c, axis=0) / total_k + eps)
-    spread = all_c.reshape(n_i * n_j, n_k, deep_k // (n_i * n_j), rank)
-    raw_c = lax.dynamic_index_in_dim(spread, me_k, 1, keepdims=False).reshape(deep_k, rank)
+    raw_c = lax.dynamic_slice_in_dim(all_c, me_k * deep_k, deep_k, 0)
     refit_c = raw_c / scale_c
     return (factor_a, refit_b, refit_c)
 

time: 167 us -> 162 us (0.970)
  blocking collectives: 14.6 us -> 0 us
  starting transfers between devices: 55.7 us -> 64.3 us
  waiting for transfers between devices: 23.3 us -> 27 us
  local copies, waits for them, and re-layouts: 4.51 us -> 2.22 us
    all_to_all x1 -> x0, blocking collectives: 14.6 us -> none  [scatter_sum(): return jnp.sum(lax.all_to_all(pieces, axes, 0, 0), axis=0)]
    all_to_all x1 -> x2, starting transfers between devices: 6.8 us -> 14.9 us  [scatter_sum(): return jnp.sum(lax.all_to_all(pieces, axes, 0, 0), axis=0)]
    all_to_all x4 -> x3, starting transfers between devices: 22.4 us -> 14.4 us  [gather_rows(): lax.all_to_all(copies, axes, 0, 0).reshape(n * x.shape[0], x.shape[1])]
    all_to_all x0 -> x1, starting transfers between devices: none -> 5.39 us  [local(): moment_b = jnp.sum(lax.all_to_all(partial_b, ('ia', 'ka'), 0, 0), axis=0)]
    all_to_all x1 -> x2, waiting for transfers between devices: 3.08 us -> 6.68 us  [scatter_sum(): return jnp.sum(lax.all_to_all(pieces, axes, 0, 0), axis=0)]
    ppermute x0 -> x1, starting transfers between devices: none -> 2.71 us  [local(): other = lax.ppermute(part, 'ia', [(i, i ^ 1) for i in range(n_i)])]
    ppermute x3, starting transfers between devices: 5.19 us -> 7.82 us  [add_partner(): return x + lax.ppermute(x, axis, [(i, i ^ step) for i in range(n)])]
    ppermute x12, starting transfers between devices: 21.4 us -> 19 us  [sum_along(): parts.append(lax.ppermute(x, 'ja', pairs))]
  transfers between devices with their start and end apart: 20 -> 22, of which waited for: 7 -> 7; matrix products, arithmetic and copies ran while one was open for 2% -> 1% of each run, Pallas kernels for 37% -> 38%
where the time goes in v2:
time: 162 us; the launch traced here: 161 us
  starting transfers between devices  64.3 us (40%)
  Pallas kernels  61.2 us (38%)
  waiting for transfers between devices  27 us (17%)
  matrix products  4.17 us (3%)
  local copies, waits for them, and re-layouts  2.22 us (1%)
    pallas_call x4, Pallas kernels, inverse_of(): pl.pallas_call(functools.partial(inverse_kernel, first, last), out_shape=...  34.7 us
    pallas_call x3, Pallas kernels, tensor_pass(): pl.pallas_call(kernel, out_shape=jax.ShapeDtypeStruct(shape, jnp.float32)...  26.4 us
    ppermute x12, starting transfers between devices, sum_along(): parts.append(lax.ppermute(x, 'ja', pairs))  19 us
    all_to_all x3, waiting for transfers between devices, gather_rows(): lax.all_to_all(copies, axes, 0, 0).reshape(n * x.shape[0], x.shape[1])  15 us
    all_to_all x2, starting transfers between devices, scatter_sum(): return jnp.sum(lax.all_to_all(pieces, axes, 0, 0), axis=0)  14.9 us
    all_to_all x3, starting transfers between devices, gather_rows(): lax.all_to_all(copies, axes, 0, 0).reshape(n * x.shape[0], x.shape[1])  14.4 us
    ppermute x3, starting transfers between devices, add_partner(): return x + lax.ppermute(x, axis, [(i, i ^ step) for i in range(n)])  7.82 us
    all_to_all x2, waiting for transfers between devices, scatter_sum(): return jnp.sum(lax.all_to_all(pieces, axes, 0, 0), axis=0)  6.68 us
  transfers between devices with their start and end apart: 22, of which 7 were waited for; matrix products, arithmetic and copies ran while one was open for 1% of the time, Pallas kernels for 38%

profile of v2, /device:TPU:1, one launch (start us, length us, event | category | flops | bytes accessed | tf_op | source)
XLA Modules:
  0.0 161.3 jit_solution(7854557519961397252)
XLA Ops:
  0.7 1.3 fusion.4
  2.0 4.7 %collective-permute-start.2 = (f32[128,256]{1,0:T(8,128)S(1)}, f32[128,256]{1,0:T(8,128)S(1)}, u32[]{:S(2)}, u32[]{:S(2)}) collective-permute-start(f32[128,256]{1,0:T(8,128)S(1)} %fusion.4), channel_id=1, source_target_pairs={{0,24},{2,26},{4,28},{6,30},{8,0},{10,2},{12,4},{14,6},{16,8},{18,... | collective-permute-start | bytes 393224 | tf_op jit(solution)/shard_map/ppermute | solution.py:215
  6.6 1.3 collective-permute-start
  7.9 8.8 %first.1 = f32[256,256]{1,0:T(8,128)} custom-call(bf16[256,128,256]{2,1,0:T(8,128)(2,1)} %t_ref.5, f32[128,256]{1,0:T(8,128)} %b_ref.1, f32[256,256]{1,0:T(8,128)} %c_ref.3), custom_call_target="tpu_custom_call" | custom-call | flops 4294967296 | bytes 16777216 | tf_op jit(solution)/shard_map/first/pallas_call | solution.py:307
  16.8 2.8 %collective-permute-start.5 = (f32[128,256]{1,0:T(8,128)S(1)}, f32[128,256]{1,0:T(8,128)S(1)}, u32[]{:S(2)}, u32[]{:S(2)}) collective-permute-start(f32[128,256]{1,0:T(8,128)S(1)} %add_add_fusion.3), channel_id=1, source_target_pairs={{0,6},{2,0},{4,2},{6,4},{8,14},{10,8},{12,10},{14,12},{16,22},{18,... | collective-permute-start | bytes 393224 | tf_op jit(solution)/shard_map/ppermute | solution.py:215
  19.6 1.6 %collective-permute-start.3 = (f32[128,256]{1,0:T(8,128)S(1)}, f32[128,256]{1,0:T(8,128)S(1)}, u32[]{:S(2)}, u32[]{:S(2)}) collective-permute-start(f32[128,256]{1,0:T(8,128)S(1)} %add_add_fusion.3), channel_id=1, source_target_pairs={{0,4},{2,6},{4,0},{6,2},{8,12},{10,14},{12,8},{14,10},{16,20},{18,... | collective-permute-start | bytes 393224 | tf_op jit(solution)/shard_map/ppermute | solution.py:215
  21.2 7.4 %all-to-all-start = ((f32[32,8,256]{2,1,0:T(8,128)}), f32[32,8,256]{2,1,0:T(8,128)S(1)}, u32[]{:S(2)}, u32[]{:S(2)}) async-start(f32[32,8,256]{2,1,0:T(8,128)} %bitcast.21), calls=%async_computation | async-start | bytes 524288 | tf_op jit(solution)/shard_map/all_to_all | solution.py:193
  28.7 2.7 %collective-permute-start.6 = (f32[128,256]{1,0:T(8,128)S(1)}, f32[128,256]{1,0:T(8,128)S(1)}, u32[]{:S(2)}, u32[]{:S(2)}) collective-permute-start(f32[128,256]{1,0:T(8,128)S(1)} %add_add_fusion.2), channel_id=1, source_target_pairs={{0,32},{32,0},{64,96},{96,64},{1,33},{33,1},{65,97},{97,65},{2,34}... | collective-permute-start | bytes 393224 | tf_op jit(solution)/shard_map/ppermute | solution.py:343
  32.1 3.1 %collective-permute-start.7 = (f32[256,256]{1,0:T(8,128)S(1)}, f32[256,256]{1,0:T(8,128)S(1)}, u32[]{:S(2)}, u32[]{:S(2)}) collective-permute-start(f32[256,256]{1,0:T(8,128)S(1)} %fusion.8), channel_id=1, source_target_pairs={{0,1},{1,0},{2,3},{3,2},{4,5},{5,4},{6,7},{7,6},{8,9},{9,8},{10,11... | collective-permute-start | bytes 786440 | tf_op jit(solution)/shard_map/ppermute | solution.py:204
  35.2 3.4 %all-to-all-done = f32[32,8,256]{2,1,0:T(8,128)S(1)} async-done(((f32[32,8,256]{2,1,0:T(8,128)}), f32[32,8,256]{2,1,0:T(8,128)S(1)}, u32[]{:S(2)}, u32[]{:S(2)}) %all-to-all-start) | async-done | bytes 262176 | tf_op jit(solution)/shard_map/all_to_all | solution.py:193
  39.3 3.9 %all-to-all-start.1 = ((f32[32,8,256]{2,1,0:T(8,128)}), f32[32,8,256]{2,1,0:T(8,128)S(1)}, u32[]{:S(2)}, u32[]{:S(2)}) async-start(f32[32,8,256]{2,1,0:T(8,128)} %broadcast_in_dim.10), calls=%async_computation.1 | async-start | bytes 524288 | tf_op jit(solution)/shard_map/all_to_all | solution.py:199
  43.3 11.4 %inverse.4 = f32[256,256]{1,0:T(8,128)S(1)} custom-call(f32[256,256]{1,0:T(8,128)S(1)} %pad_maximum_fusion.one_ref, f32[256,256]{1,0:T(8,128)S(1)} %add.80.two_ref), custom_call_target="tpu_custom_call" | custom-call | flops 17179869184 | bytes 786432 | tf_op jit(solution)/shard_map/inverse/pallas_call | solution.py:176
  55.8 4.3 %collective-permute-start.8 = (f32[256,256]{1,0:T(8,128)S(1)}, f32[256,256]{1,0:T(8,128)S(1)}, u32[]{:S(2)}, u32[]{:S(2)}) collective-permute-start(f32[256,256]{1,0:T(8,128)S(1)} %fusion.9), channel_id=1, source_target_pairs={{0,32},{32,0},{64,96},{96,64},{1,33},{33,1},{65,97},{97,65},{2,34}... | collective-permute-start | bytes 786440 | tf_op jit(solution)/shard_map/ppermute | solution.py:204
  60.1 9.1 %second.1 = f32[8,128,256]{2,1,0:T(8,128)} custom-call(bf16[256,128,256]{2,1,0:T(8,128)(2,1)} %t_ref.5, f32[256,256]{1,0:T(8,128)S(1)} %fusion.1.a_ref, f32[256,256]{1,0:T(8,128)S(1)} %copy-done), custom_call_target="tpu_custom_call" | custom-call | flops 4294967296 | bytes 16777216 | tf_op jit(solution)/shard_map/second/pallas_call | solution.py:307
  69.6 5.4 %all-to-all-start.2 = ((f32[8,128,256]{2,1,0:T(8,128)}), f32[8,128,256]{2,1,0:T(8,128)S(1)}, u32[]{:S(2)}, u32[]{:S(2)}) async-start(f32[8,128,256]{2,1,0:T(8,128)} %second.1), calls=%async_computation.2 | async-start | bytes 2097152 | tf_op jit(solution)/shard_map/all_to_all | solution.py:358
  75.0 2.2 %collective-permute-done.9 = f32[256,256]{1,0:T(8,128)S(1)} collective-permute-done((f32[256,256]{1,0:T(8,128)S(1)}, f32[256,256]{1,0:T(8,128)S(1)}, u32[]{:S(2)}, u32[]{:S(2)}) %collective-permute-start.9) | collective-permute-done | bytes 262176 | tf_op jit(solution)/shard_map/ppermute | solution.py:204
  77.3 11.4 %inverse.5 = f32[256,256]{1,0:T(8,128)S(1)} custom-call(f32[256,256]{1,0:T(8,128)S(1)} %get-tuple-element.26.one_ref, f32[256,256]{1,0:T(8,128)S(1)} %add.80.two_ref), custom_call_target="tpu_custom_call" | custom-call | flops 17179869184 | bytes 786432 | tf_op jit(solution)/shard_map/inverse/pallas_call | solution.py:176
  88.7 1.3 all-to-all-done.2
  90.8 2.6 %collective-permute-start.12 = (f32[256,256]{1,0:T(8,128)S(1)}, f32[256,256]{1,0:T(8,128)S(1)}, u32[]{:S(2)}, u32[]{:S(2)}) collective-permute-start(f32[256,256]{1,0:T(8,128)S(1)} %fusion.10), channel_id=1, source_target_pairs={{0,24},{2,26},{4,28},{6,30},{8,0},{10,2},{12,4},{14,6},{16,8},{18,... | collective-permute-start | bytes 786440 | tf_op jit(solution)/shard_map/ppermute | solution.py:215
  93.4 1.7 %collective-permute-start.10 = (f32[256,256]{1,0:T(8,128)S(1)}, f32[256,256]{1,0:T(8,128)S(1)}, u32[]{:S(2)}, u32[]{:S(2)}) collective-permute-start(f32[256,256]{1,0:T(8,128)S(1)} %fusion.10), channel_id=1, source_target_pairs={{0,16},{2,18},{4,20},{6,22},{8,24},{10,26},{12,28},{14,30},{16,0},... | collective-permute-start | bytes 786440 | tf_op jit(solution)/shard_map/ppermute | solution.py:215
  95.7 5.4 %all-to-all-start.3 = ((f32[16,1,256]{2,1,0:T(1,128)}), f32[16,1,256]{2,1,0:T(1,128)S(1)}, u32[]{:S(2)}, u32[]{:S(2)}) async-start(f32[16,1,256]{2,1,0:T(1,128)} %broadcast_in_dim.12), calls=%async_computation.3 | async-start | bytes 32768 | tf_op jit(solution)/shard_map/all_to_all | solution.py:199
  101.1 6.7 %all-to-all-done.3 = f32[16,1,256]{2,1,0:T(1,128)S(1)} async-done(((f32[16,1,256]{2,1,0:T(1,128)}), f32[16,1,256]{2,1,0:T(1,128)S(1)}, u32[]{:S(2)}, u32[]{:S(2)}) %all-to-all-start.3) | async-done | bytes 16416 | tf_op jit(solution)/shard_map/all_to_all | solution.py:199
  108.0 2.5 %collective-permute-start.15 = (f32[256,256]{1,0:T(8,128)S(1)}, f32[256,256]{1,0:T(8,128)S(1)}, u32[]{:S(2)}, u32[]{:S(2)}) collective-permute-start(f32[256,256]{1,0:T(8,128)S(1)} %add_add_fusion.1), channel_id=1, source_target_pairs={{0,6},{2,0},{4,2},{6,4},{8,14},{10,8},{12,10},{14,12},{16,22},{18,... | collective-permute-start | bytes 786440 | tf_op jit(solution)/shard_map/ppermute | solution.py:215
  110.6 1.8 %collective-permute-start.13 = (f32[256,256]{1,0:T(8,128)S(1)}, f32[256,256]{1,0:T(8,128)S(1)}, u32[]{:S(2)}, u32[]{:S(2)}) collective-permute-start(f32[256,256]{1,0:T(8,128)S(1)} %add_add_fusion.1), channel_id=1, source_target_pairs={{0,4},{2,6},{4,0},{6,2},{8,12},{10,14},{12,8},{14,10},{16,20},{18,... | collective-permute-start | bytes 786440 | tf_op jit(solution)/shard_map/ppermute | solution.py:215
  112.4 8.6 %third.1 = f32[64,8,128]{2,1,0:T(8,128)} custom-call(bf16[256,128,256]{2,1,0:T(8,128)(2,1)} %t_ref.5, f32[256,256]{1,0:T(8,128)S(1)} %broadcast_divide_fusion.a_ref, f32[128,256]{1,0:T(8,128)S(1)} %broadcast_divide_fusion.1.b_ref), custom_call_target="tpu_custom_call" | custom-call | flops 4294967296 | bytes 16777216 | tf_op jit(solution)/shard_map/third/pallas_call | solution.py:307
  121.0 1.8 %collective-permute-done.13 = f32[256,256]{1,0:T(8,128)S(1)} collective-permute-done((f32[256,256]{1,0:T(8,128)S(1)}, f32[256,256]{1,0:T(8,128)S(1)}, u32[]{:S(2)}, u32[]{:S(2)}) %collective-permute-start.13) | collective-permute-done | bytes 262176 | tf_op jit(solution)/shard_map/ppermute | solution.py:215
  122.9 7.5 %all-to-all-start.4 = ((f32[64,8,128]{2,1,0:T(8,128)}), f32[64,8,128]{2,1,0:T(8,128)S(1)}, u32[]{:S(2)}, u32[]{:S(2)}) async-start(f32[64,8,128]{2,1,0:T(8,128)} %third.1), calls=%async_computation.4 | async-start | bytes 524288 | tf_op jit(solution)/shard_map/all_to_all | solution.py:193
  130.4 6.0 %inverse.6.rest_0_ = f32[256,256]{1,0:T(8,128)S(1)} custom-call(f32[256,256]{1,0:T(8,128)S(1)} %get-tuple-element.26.one_ref, f32[256,256]{1,0:T(8,128)S(1)} %add_add_fusion.two_ref), custom_call_target="tpu_custom_call" | custom-call | flops 8589934592 | bytes 786432 | tf_op jit(solution)/shard_map/inverse/pallas_call | solution.py:176
  136.4 3.3 %all-to-all-done.4 = f32[64,8,128]{2,1,0:T(8,128)S(1)} async-done(((f32[64,8,128]{2,1,0:T(8,128)}), f32[64,8,128]{2,1,0:T(8,128)S(1)}, u32[]{:S(2)}, u32[]{:S(2)}) %all-to-all-start.4) | async-done | bytes 262176 | tf_op jit(solution)/shard_map/all_to_all | solution.py:193
  140.6 5.2 %all-to-all-start.5 = ((f32[128,8,128]{2,1,0:T(8,128)}), f32[128,8,128]{2,1,0:T(8,128)S(1)}, u32[]{:S(2)}, u32[]{:S(2)}) async-start(f32[128,8,128]{2,1,0:T(8,128)} %broadcast_in_dim.13), calls=%async_computation.5 | async-start | bytes 1048576 | tf_op jit(solution)/shard_map/all_to_all | solution.py:199
  145.8 5.8 %inverse.7 = f32[256,256]{1,0:T(8,128)S(1)} custom-call(f32[256,256]{1,0:T(8,128)S(1)} %get-tuple-element.26.one_ref, f32[256,256]{1,0:T(8,128)S(1)} %add_add_fusion.two_ref, f32[256,256]{1,0:T(8,128)S(1)} %inverse.6.rest_0_), custom_call_target="tpu_custom_call" | custom-call | flops 8589934592 | bytes 786432 | tf_op jit(solution)/shard_map/inverse/pallas_call | solution.py:176
  151.7 8.3 %all-to-all-done.5 = f32[128,8,128]{2,1,0:T(8,128)S(1)} async-done(((f32[128,8,128]{2,1,0:T(8,128)}), f32[128,8,128]{2,1,0:T(8,128)S(1)}, u32[]{:S(2)}, u32[]{:S(2)}) %all-to-all-start.5) | async-done | bytes 524320 | tf_op jit(solution)/shard_map/all_to_all | solution.py:199
  (56 shorter events, 6.9 us)
Async XLA Ops:
  0.6 30.8 %copy-start = (f32[256,256]{1,0:T(8,128)S(1)}, f32[256,256]{1,0:T(8,128)}, u32[]{:S(2)}) copy-start(f32[256,256]{1,0:T(8,128)} %c_ref.3) | copy-start | bytes 786436
  2.0 14.8 %collective-permute-start.2 = (f32[128,256]{1,0:T(8,128)S(1)}, f32[128,256]{1,0:T(8,128)S(1)}, u32[]{:S(2)}, u32[]{:S(2)}) collective-permute-start(f32[128,256]{1,0:T(8,128)S(1)} %fusion.4), channel_id=1, source_target_pairs={{0,24},{2,26},{4,28},{6,30},{8,0},{10,2},{12,4},{14,6},{16,8},{18,... | collective-permute-start | bytes 393224 | tf_op jit(solution)/shard_map/ppermute | solution.py:215
  6.6 10.1 %collective-permute-start.1 = (f32[128,256]{1,0:T(8,128)S(1)}, f32[128,256]{1,0:T(8,128)S(1)}, u32[]{:S(2)}, u32[]{:S(2)}) collective-permute-start(f32[128,256]{1,0:T(8,128)S(1)} %fusion.4), channel_id=1, source_target_pairs={{0,8},{2,10},{4,12},{6,14},{8,16},{10,18},{12,20},{14,22},{16,24},... | collective-permute-start | bytes 393224 | tf_op jit(solution)/shard_map/ppermute | solution.py:215
  6.6 10.1 %collective-permute-start = (f32[128,256]{1,0:T(8,128)S(1)}, f32[128,256]{1,0:T(8,128)S(1)}, u32[]{:S(2)}, u32[]{:S(2)}) collective-permute-start(f32[128,256]{1,0:T(8,128)S(1)} %fusion.4), channel_id=1, source_target_pairs={{0,16},{2,18},{4,20},{6,22},{8,24},{10,26},{12,28},{14,30},{16,0},... | collective-permute-start | bytes 393224 | tf_op jit(solution)/shard_map/ppermute | solution.py:215
  16.8 11.9 %collective-permute-start.5 = (f32[128,256]{1,0:T(8,128)S(1)}, f32[128,256]{1,0:T(8,128)S(1)}, u32[]{:S(2)}, u32[]{:S(2)}) collective-permute-start(f32[128,256]{1,0:T(8,128)S(1)} %add_add_fusion.3), channel_id=1, source_target_pairs={{0,6},{2,0},{4,2},{6,4},{8,14},{10,8},{12,10},{14,12},{16,22},{18,... | collective-permute-start | bytes 393224 | tf_op jit(solution)/shard_map/ppermute | solution.py:215
  19.6 9.1 %collective-permute-start.4 = (f32[128,256]{1,0:T(8,128)S(1)}, f32[128,256]{1,0:T(8,128)S(1)}, u32[]{:S(2)}, u32[]{:S(2)}) collective-permute-start(f32[128,256]{1,0:T(8,128)S(1)} %add_add_fusion.3), channel_id=1, source_target_pairs={{0,2},{2,4},{4,6},{6,0},{8,10},{10,12},{12,14},{14,8},{16,18},{18,... | collective-permute-start | bytes 393224 | tf_op jit(solution)/shard_map/ppermute | solution.py:215
  19.6 9.1 %collective-permute-start.3 = (f32[128,256]{1,0:T(8,128)S(1)}, f32[128,256]{1,0:T(8,128)S(1)}, u32[]{:S(2)}, u32[]{:S(2)}) collective-permute-start(f32[128,256]{1,0:T(8,128)S(1)} %add_add_fusion.3), channel_id=1, source_target_pairs={{0,4},{2,6},{4,0},{6,2},{8,12},{10,14},{12,8},{14,10},{16,20},{18,... | collective-permute-start | bytes 393224 | tf_op jit(solution)/shard_map/ppermute | solution.py:215
  21.2 17.3 %all-to-all-start = ((f32[32,8,256]{2,1,0:T(8,128)}), f32[32,8,256]{2,1,0:T(8,128)S(1)}, u32[]{:S(2)}, u32[]{:S(2)}) async-start(f32[32,8,256]{2,1,0:T(8,128)} %bitcast.21), calls=%async_computation | async-start | bytes 524288 | tf_op jit(solution)/shard_map/all_to_all | solution.py:193
  28.7 14.5 %collective-permute-start.6 = (f32[128,256]{1,0:T(8,128)S(1)}, f32[128,256]{1,0:T(8,128)S(1)}, u32[]{:S(2)}, u32[]{:S(2)}) collective-permute-start(f32[128,256]{1,0:T(8,128)S(1)} %add_add_fusion.2), channel_id=1, source_target_pairs={{0,32},{32,0},{64,96},{96,64},{1,33},{33,1},{65,97},{97,65},{2,34}... | collective-permute-start | bytes 393224 | tf_op jit(solution)/shard_map/ppermute | solution.py:343
  32.1 11.2 %collective-permute-start.7 = (f32[256,256]{1,0:T(8,128)S(1)}, f32[256,256]{1,0:T(8,128)S(1)}, u32[]{:S(2)}, u32[]{:S(2)}) collective-permute-start(f32[256,256]{1,0:T(8,128)S(1)} %fusion.8), channel_id=1, source_target_pairs={{0,1},{1,0},{2,3},{3,2},{4,5},{5,4},{6,7},{7,6},{8,9},{9,8},{10,11... | collective-permute-start | bytes 786440 | tf_op jit(solution)/shard_map/ppermute | solution.py:204
  39.3 15.5 %all-to-all-start.1 = ((f32[32,8,256]{2,1,0:T(8,128)}), f32[32,8,256]{2,1,0:T(8,128)S(1)}, u32[]{:S(2)}, u32[]{:S(2)}) async-start(f32[32,8,256]{2,1,0:T(8,128)} %broadcast_in_dim.10), calls=%async_computation.1 | async-start | bytes 524288 | tf_op jit(solution)/shard_map/all_to_all | solution.py:199
  55.8 13.4 %collective-permute-start.8 = (f32[256,256]{1,0:T(8,128)S(1)}, f32[256,256]{1,0:T(8,128)S(1)}, u32[]{:S(2)}, u32[]{:S(2)}) collective-permute-start(f32[256,256]{1,0:T(8,128)S(1)} %fusion.9), channel_id=1, source_target_pairs={{0,32},{32,0},{64,96},{96,64},{1,33},{33,1},{65,97},{97,65},{2,34}... | collective-permute-start | bytes 786440 | tf_op jit(solution)/shard_map/ppermute | solution.py:204
  69.2 8.0 %collective-permute-start.9 = (f32[256,256]{1,0:T(8,128)S(1)}, f32[256,256]{1,0:T(8,128)S(1)}, u32[]{:S(2)}, u32[]{:S(2)}) collective-permute-start(f32[256,256]{1,0:T(8,128)S(1)} %add.81), channel_id=1, source_target_pairs={{0,64},{32,96},{64,0},{96,32},{1,65},{33,97},{65,1},{97,33},{2,66}... | collective-permute-start | bytes 786440 | tf_op jit(solution)/shard_map/ppermute | solution.py:204
  69.6 20.4 %all-to-all-start.2 = ((f32[8,128,256]{2,1,0:T(8,128)}), f32[8,128,256]{2,1,0:T(8,128)S(1)}, u32[]{:S(2)}, u32[]{:S(2)}) async-start(f32[8,128,256]{2,1,0:T(8,128)} %second.1), calls=%async_computation.2 | async-start | bytes 2097152 | tf_op jit(solution)/shard_map/all_to_all | solution.py:358
  90.8 17.1 %collective-permute-start.12 = (f32[256,256]{1,0:T(8,128)S(1)}, f32[256,256]{1,0:T(8,128)S(1)}, u32[]{:S(2)}, u32[]{:S(2)}) collective-permute-start(f32[256,256]{1,0:T(8,128)S(1)} %fusion.10), channel_id=1, source_target_pairs={{0,24},{2,26},{4,28},{6,30},{8,0},{10,2},{12,4},{14,6},{16,8},{18,... | collective-permute-start | bytes 786440 | tf_op jit(solution)/shard_map/ppermute | solution.py:215
  93.4 14.5 %collective-permute-start.11 = (f32[256,256]{1,0:T(8,128)S(1)}, f32[256,256]{1,0:T(8,128)S(1)}, u32[]{:S(2)}, u32[]{:S(2)}) collective-permute-start(f32[256,256]{1,0:T(8,128)S(1)} %fusion.10), channel_id=1, source_target_pairs={{0,8},{2,10},{4,12},{6,14},{8,16},{10,18},{12,20},{14,22},{16,24},... | collective-permute-start | bytes 786440 | tf_op jit(solution)/shard_map/ppermute | solution.py:215
  93.4 14.5 %collective-permute-start.10 = (f32[256,256]{1,0:T(8,128)S(1)}, f32[256,256]{1,0:T(8,128)S(1)}, u32[]{:S(2)}, u32[]{:S(2)}) collective-permute-start(f32[256,256]{1,0:T(8,128)S(1)} %fusion.10), channel_id=1, source_target_pairs={{0,16},{2,18},{4,20},{6,22},{8,24},{10,26},{12,28},{14,30},{16,0},... | collective-permute-start | bytes 786440 | tf_op jit(solution)/shard_map/ppermute | solution.py:215
  95.7 12.1 %all-to-all-start.3 = ((f32[16,1,256]{2,1,0:T(1,128)}), f32[16,1,256]{2,1,0:T(1,128)S(1)}, u32[]{:S(2)}, u32[]{:S(2)}) async-start(f32[16,1,256]{2,1,0:T(1,128)} %broadcast_in_dim.12), calls=%async_computation.3 | async-start | bytes 32768 | tf_op jit(solution)/shard_map/all_to_all | solution.py:199
  101.1 35.3 %copy-start.1 = (f32[256,256]{1,0:T(8,128)}, f32[256,256]{1,0:T(8,128)S(1)}, u32[]{:S(2)}) copy-start(f32[256,256]{1,0:T(8,128)S(1)} %broadcast_divide_fusion.a_ref) | copy-start | bytes 786436
  108.0 12.9 %collective-permute-start.15 = (f32[256,256]{1,0:T(8,128)S(1)}, f32[256,256]{1,0:T(8,128)S(1)}, u32[]{:S(2)}, u32[]{:S(2)}) collective-permute-start(f32[256,256]{1,0:T(8,128)S(1)} %add_add_fusion.1), channel_id=1, source_target_pairs={{0,6},{2,0},{4,2},{6,4},{8,14},{10,8},{12,10},{14,12},{16,22},{18,... | collective-permute-start | bytes 786440 | tf_op jit(solution)/shard_map/ppermute | solution.py:215
  110.6 10.4 %collective-permute-start.14 = (f32[256,256]{1,0:T(8,128)S(1)}, f32[256,256]{1,0:T(8,128)S(1)}, u32[]{:S(2)}, u32[]{:S(2)}) collective-permute-start(f32[256,256]{1,0:T(8,128)S(1)} %add_add_fusion.1), channel_id=1, source_target_pairs={{0,2},{2,4},{4,6},{6,0},{8,10},{10,12},{12,14},{14,8},{16,18},{18,... | collective-permute-start | bytes 786440 | tf_op jit(solution)/shard_map/ppermute | solution.py:215
  110.6 12.2 %collective-permute-start.13 = (f32[256,256]{1,0:T(8,128)S(1)}, f32[256,256]{1,0:T(8,128)S(1)}, u32[]{:S(2)}, u32[]{:S(2)}) collective-permute-start(f32[256,256]{1,0:T(8,128)S(1)} %add_add_fusion.1), channel_id=1, source_target_pairs={{0,4},{2,6},{4,0},{6,2},{8,12},{10,14},{12,8},{14,10},{16,20},{18,... | collective-permute-start | bytes 786440 | tf_op jit(solution)/shard_map/ppermute | solution.py:215
  112.4 24.1 %copy-start.2 = (f32[128,256]{1,0:T(8,128)}, f32[128,256]{1,0:T(8,128)S(1)}, u32[]{:S(2)}) copy-start(f32[128,256]{1,0:T(8,128)S(1)} %broadcast_divide_fusion.1.b_ref) | copy-start | bytes 393220
  122.9 16.8 %all-to-all-start.4 = ((f32[64,8,128]{2,1,0:T(8,128)}), f32[64,8,128]{2,1,0:T(8,128)S(1)}, u32[]{:S(2)}, u32[]{:S(2)}) async-start(f32[64,8,128]{2,1,0:T(8,128)} %third.1), calls=%async_computation.4 | async-start | bytes 524288 | tf_op jit(solution)/shard_map/all_to_all | solution.py:193
  140.6 19.3 %all-to-all-start.5 = ((f32[128,8,128]{2,1,0:T(8,128)}), f32[128,8,128]{2,1,0:T(8,128)S(1)}, u32[]{:S(2)}, u32[]{:S(2)}) async-start(f32[128,8,128]{2,1,0:T(8,128)} %broadcast_in_dim.13), calls=%async_computation.5 | async-start | bytes 1048576 | tf_op jit(solution)/shard_map/all_to_all | solution.py:199

commit v3 on v2

--- a/solution.py
+++ b/solution.py
@@ -216,6 +216,15 @@
     return (x + parts[1]) + (parts[0] + parts[2])
 
 
+def whole_of(part):
+    n = lax.axis_size("ia")
+    other = lax.ppermute(part, "ia", [(i, i ^ 1) for i in range(n)])
+    first = lax.axis_index("ia") % 2 == 0
+    return jnp.concatenate(
+        [jnp.where(first, part, other), jnp.where(first, other, part)], axis=0
+    )
+
+
 def diagonal_of(square):
     n = square.shape[0]
     return jnp.sum(jnp.where(jnp.eye(n, dtype=bool), square, 0.0), axis=0)
@@ -340,10 +349,7 @@
     part, late_c, partial_a = lax.optimization_barrier((part, factor_c, partial_a))
     part = sum_along(part, 1)
     gram_c = add_partner(gram_of(late_c), "ka", 1)
-    other = lax.ppermute(part, "ia", [(i, i ^ 1) for i in range(n_i)])
-    gram_b = jnp.concatenate(
-        [jnp.where(core == 0, part, other), jnp.where(core == 0, other, part)], axis=0
-    )
+    gram_b = whole_of(part)
     shared_a = scatter_sum(partial_a, ("ja", "ka"))
     moment_a = gather_rows(shared_a, ("ja", "ka"))
     raw_a = product(moment_a, inverse_of(gram_b, gram_c))
@@ -359,9 +365,8 @@
     raw_b = product(moment_b, inverse_of(raw_gram_a, gram_c)) * scale_a
     sums_b = jnp.sum(gather_rows(jnp.sum(raw_b * raw_b, axis=0, keepdims=True), "ja"), axis=0)
     scale_b = jnp.sqrt(sums_b / total_j + eps)
-    raw_gram_b = sum_along(gram_of(raw_b), 0)
-    scale_b, raw_gram_b = lax.optimization_barrier((scale_b, raw_gram_b))
-    raw_gram_b = sum_along(raw_gram_b, 1)
+    own = lax.dynamic_slice_in_dim(raw_b, core * half, half, 1)
+    part = sum_along(sum_along(product(own.T, raw_b), 0), 1)
     refit_b = raw_b / scale_b
 
     down, across = deep_k // 8, rank // 128
@@ -374,7 +379,8 @@
         "third",
         [pltpu.VMEM((deep_k, rank), jnp.float32)],
     )
-    raw_gram_b, partial_c = lax.optimization_barrier((raw_gram_b, partial_c))
+    part, partial_c = lax.optimization_barrier((part, partial_c))
+    raw_gram_b = whole_of(part)
     shared_c = scatter_sum(partial_c.reshape(-1, 128), ("ia", "ja"))
     middle = rank // PANEL // 2
     state = inverse_of(raw_gram_a, raw_gram_b, 0, middle)

time: 162 us -> 161 us (level)
  waiting for transfers between devices: 27 us -> 23.5 us
  starting transfers between devices: 64.3 us -> 67.6 us
    all_to_all x3, waiting for transfers between devices: 15 us -> 9.96 us  [gather_rows(): lax.all_to_all(copies, axes, 0, 0).reshape(n * x.shape[0], x.shape[1])]
    ppermute x1 -> x2, starting transfers between devices: 2.71 us -> 6.41 us  [whole_of(): other = lax.ppermute(part, 'ia', [(i, i ^ 1) for i in range(n)])]
    all_to_all x2, starting transfers between devices: 14.9 us -> 11.6 us  [scatter_sum(): return jnp.sum(lax.all_to_all(pieces, axes, 0, 0), axis=0)]
    all_to_all x3, starting transfers between devices: 14.4 us -> 17.2 us  [gather_rows(): lax.all_to_all(copies, axes, 0, 0).reshape(n * x.shape[0], x.shape[1])]
    ppermute x12, waiting for transfers between devices: 1.88 us -> 3.52 us  [sum_along(): parts.append(lax.ppermute(x, 'ja', pairs))]
  transfers between devices with their start and end apart: 22 -> 23, of which waited for: 7 -> 7; matrix products, arithmetic and copies ran while one was open for 1% -> 1% of each run, Pallas kernels for 38% -> 38%
where the time goes in v3:
time: 161 us
  starting transfers between devices  67.6 us (42%)
  Pallas kernels  61.1 us (38%)
  waiting for transfers between devices  23.5 us (15%)
  matrix products  4.07 us (3%)
  local copies, waits for them, and re-layouts  2.22 us (1%)
    pallas_call x4, Pallas kernels, inverse_of(): pl.pallas_call(functools.partial(inverse_kernel, first, last), out_shape=...  34.7 us
    pallas_call x3, Pallas kernels, tensor_pass(): pl.pallas_call(kernel, out_shape=jax.ShapeDtypeStruct(shape, jnp.float32)...  26.4 us
    ppermute x12, starting transfers between devices, sum_along(): parts.append(lax.ppermute(x, 'ja', pairs))  19.1 us
    all_to_all x3, starting transfers between devices, gather_rows(): lax.all_to_all(copies, axes, 0, 0).reshape(n * x.shape[0], x.shape[1])  17.2 us
    all_to_all x2, starting transfers between devices, scatter_sum(): return jnp.sum(lax.all_to_all(pieces, axes, 0, 0), axis=0)  11.6 us
    all_to_all x3, waiting for transfers between devices, gather_rows(): lax.all_to_all(copies, axes, 0, 0).reshape(n * x.shape[0], x.shape[1])  9.96 us
    ppermute x3, starting transfers between devices, add_partner(): return x + lax.ppermute(x, axis, [(i, i ^ step) for i in range(n)])  7.86 us
    all_to_all x2, waiting for transfers between devices, scatter_sum(): return jnp.sum(lax.all_to_all(pieces, axes, 0, 0), axis=0)  6.6 us
  transfers between devices with their start and end apart: 23, of which 7 were waited for; matrix products, arithmetic and copies ran while one was open for 1% of the time, Pallas kernels for 38%

profile of v3, /device:TPU:1, one launch (start us, length us, event | category | flops | bytes accessed | tf_op | source)
XLA Modules:
  0.0 160.9 jit_solution(15003180640681256407)
XLA Ops:
  0.7 1.3 fusion.6
  2.0 4.7 %collective-permute-start.2 = (f32[128,256]{1,0:T(8,128)S(1)}, f32[128,256]{1,0:T(8,128)S(1)}, u32[]{:S(2)}, u32[]{:S(2)}) collective-permute-start(f32[128,256]{1,0:T(8,128)S(1)} %fusion.6), channel_id=1, source_target_pairs={{0,24},{2,26},{4,28},{6,30},{8,0},{10,2},{12,4},{14,6},{16,8},{18,... | collective-permute-start | bytes 393224 | tf_op jit(solution)/shard_map/ppermute | solution.py:215
  6.6 1.3 collective-permute-start
  7.9 8.8 %first.1 = f32[256,256]{1,0:T(8,128)} custom-call(bf16[256,128,256]{2,1,0:T(8,128)(2,1)} %t_ref.5, f32[128,256]{1,0:T(8,128)} %b_ref.1, f32[256,256]{1,0:T(8,128)} %c_ref.3), custom_call_target="tpu_custom_call" | custom-call | flops 4294967296 | bytes 16777216 | tf_op jit(solution)/shard_map/first/pallas_call | solution.py:316
  16.8 2.8 %collective-permute-start.5 = (f32[128,256]{1,0:T(8,128)S(1)}, f32[128,256]{1,0:T(8,128)S(1)}, u32[]{:S(2)}, u32[]{:S(2)}) collective-permute-start(f32[128,256]{1,0:T(8,128)S(1)} %add_add_fusion.3), channel_id=1, source_target_pairs={{0,6},{2,0},{4,2},{6,4},{8,14},{10,8},{12,10},{14,12},{16,22},{18,... | collective-permute-start | bytes 393224 | tf_op jit(solution)/shard_map/ppermute | solution.py:215
  19.6 1.6 %collective-permute-start.3 = (f32[128,256]{1,0:T(8,128)S(1)}, f32[128,256]{1,0:T(8,128)S(1)}, u32[]{:S(2)}, u32[]{:S(2)}) collective-permute-start(f32[128,256]{1,0:T(8,128)S(1)} %add_add_fusion.3), channel_id=1, source_target_pairs={{0,4},{2,6},{4,0},{6,2},{8,12},{10,14},{12,8},{14,10},{16,20},{18,... | collective-permute-start | bytes 393224 | tf_op jit(solution)/shard_map/ppermute | solution.py:215
  21.2 7.4 %all-to-all-start = ((f32[32,8,256]{2,1,0:T(8,128)}), f32[32,8,256]{2,1,0:T(8,128)S(1)}, u32[]{:S(2)}, u32[]{:S(2)}) async-start(f32[32,8,256]{2,1,0:T(8,128)} %bitcast.20), calls=%async_computation | async-start | bytes 524288 | tf_op jit(solution)/shard_map/all_to_all | solution.py:193
  28.7 2.7 %collective-permute-start.6 = (f32[128,256]{1,0:T(8,128)S(1)}, f32[128,256]{1,0:T(8,128)S(1)}, u32[]{:S(2)}, u32[]{:S(2)}) collective-permute-start(f32[128,256]{1,0:T(8,128)S(1)} %add_add_fusion.2), channel_id=1, source_target_pairs={{0,32},{32,0},{64,96},{96,64},{1,33},{33,1},{65,97},{97,65},{2,34}... | collective-permute-start | bytes 393224 | tf_op jit(solution)/shard_map/ppermute | solution.py:221
  32.1 3.1 %collective-permute-start.7 = (f32[256,256]{1,0:T(8,128)S(1)}, f32[256,256]{1,0:T(8,128)S(1)}, u32[]{:S(2)}, u32[]{:S(2)}) collective-permute-start(f32[256,256]{1,0:T(8,128)S(1)} %fusion.11), channel_id=1, source_target_pairs={{0,1},{1,0},{2,3},{3,2},{4,5},{5,4},{6,7},{7,6},{8,9},{9,8},{10,11... | collective-permute-start | bytes 786440 | tf_op jit(solution)/shard_map/ppermute | solution.py:204
  35.2 3.4 %all-to-all-done = f32[32,8,256]{2,1,0:T(8,128)S(1)} async-done(((f32[32,8,256]{2,1,0:T(8,128)}), f32[32,8,256]{2,1,0:T(8,128)S(1)}, u32[]{:S(2)}, u32[]{:S(2)}) %all-to-all-start) | async-done | bytes 262176 | tf_op jit(solution)/shard_map/all_to_all | solution.py:193
  39.3 3.9 %all-to-all-start.1 = ((f32[32,8,256]{2,1,0:T(8,128)}), f32[32,8,256]{2,1,0:T(8,128)S(1)}, u32[]{:S(2)}, u32[]{:S(2)}) async-start(f32[32,8,256]{2,1,0:T(8,128)} %broadcast_in_dim.10), calls=%async_computation.1 | async-start | bytes 524288 | tf_op jit(solution)/shard_map/all_to_all | solution.py:199
  43.3 11.4 %inverse.4 = f32[256,256]{1,0:T(8,128)S(1)} custom-call(f32[256,256]{1,0:T(8,128)S(1)} %pad_maximum_fusion.one_ref, f32[256,256]{1,0:T(8,128)S(1)} %add.93.two_ref), custom_call_target="tpu_custom_call" | custom-call | flops 17179869184 | bytes 786432 | tf_op jit(solution)/shard_map/inverse/pallas_call | solution.py:176
  55.8 4.3 %collective-permute-start.8 = (f32[256,256]{1,0:T(8,128)S(1)}, f32[256,256]{1,0:T(8,128)S(1)}, u32[]{:S(2)}, u32[]{:S(2)}) collective-permute-start(f32[256,256]{1,0:T(8,128)S(1)} %fusion.12), channel_id=1, source_target_pairs={{0,32},{32,0},{64,96},{96,64},{1,33},{33,1},{65,97},{97,65},{2,34}... | collective-permute-start | bytes 786440 | tf_op jit(solution)/shard_map/ppermute | solution.py:204
  60.1 9.1 %second.1 = f32[8,128,256]{2,1,0:T(8,128)} custom-call(bf16[256,128,256]{2,1,0:T(8,128)(2,1)} %t_ref.5, f32[256,256]{1,0:T(8,128)S(1)} %fusion.1.a_ref, f32[256,256]{1,0:T(8,128)S(1)} %copy-done), custom_call_target="tpu_custom_call" | custom-call | flops 4294967296 | bytes 16777216 | tf_op jit(solution)/shard_map/second/pallas_call | solution.py:316
  69.7 5.3 %all-to-all-start.2 = ((f32[8,128,256]{2,1,0:T(8,128)}), f32[8,128,256]{2,1,0:T(8,128)S(1)}, u32[]{:S(2)}, u32[]{:S(2)}) async-start(f32[8,128,256]{2,1,0:T(8,128)} %second.1), calls=%async_computation.2 | async-start | bytes 2097152 | tf_op jit(solution)/shard_map/all_to_all | solution.py:364
  75.0 2.2 %collective-permute-done.9 = f32[256,256]{1,0:T(8,128)S(1)} collective-permute-done((f32[256,256]{1,0:T(8,128)S(1)}, f32[256,256]{1,0:T(8,128)S(1)}, u32[]{:S(2)}, u32[]{:S(2)}) %collective-permute-start.9) | collective-permute-done | bytes 262176 | tf_op jit(solution)/shard_map/ppermute | solution.py:204
  77.3 11.4 %inverse.5 = f32[256,256]{1,0:T(8,128)S(1)} custom-call(f32[256,256]{1,0:T(8,128)S(1)} %get-tuple-element.22.one_ref, f32[256,256]{1,0:T(8,128)S(1)} %add.93.two_ref), custom_call_target="tpu_custom_call" | custom-call | flops 17179869184 | bytes 786432 | tf_op jit(solution)/shard_map/inverse/pallas_call | solution.py:176
  91.0 6.6 %all-to-all-start.3 = ((f32[16,1,256]{2,1,0:T(1,128)}), f32[16,1,256]{2,1,0:T(1,128)S(1)}, u32[]{:S(2)}, u32[]{:S(2)}) async-start(f32[16,1,256]{2,1,0:T(1,128)} %broadcast_in_dim.12), calls=%async_computation.3 | async-start | bytes 32768 | tf_op jit(solution)/shard_map/all_to_all | solution.py:199
  97.9 2.6 %collective-permute-start.12 = (f32[128,256]{1,0:T(8,128)S(1)}, f32[128,256]{1,0:T(8,128)S(1)}, u32[]{:S(2)}, u32[]{:S(2)}) collective-permute-start(f32[128,256]{1,0:T(8,128)S(1)} %fusion.4), channel_id=1, source_target_pairs={{0,24},{2,26},{4,28},{6,30},{8,0},{10,2},{12,4},{14,6},{16,8},{18,... | collective-permute-start | bytes 393224 | tf_op jit(solution)/shard_map/ppermute | solution.py:215
  100.6 1.8 %collective-permute-start.10 = (f32[128,256]{1,0:T(8,128)S(1)}, f32[128,256]{1,0:T(8,128)S(1)}, u32[]{:S(2)}, u32[]{:S(2)}) collective-permute-start(f32[128,256]{1,0:T(8,128)S(1)} %fusion.4), channel_id=1, source_target_pairs={{0,16},{2,18},{4,20},{6,22},{8,24},{10,26},{12,28},{14,30},{16,0},... | collective-permute-start | bytes 393224 | tf_op jit(solution)/shard_map/ppermute | solution.py:215
  102.3 1.7 %all-to-all-done.3 = f32[16,1,256]{2,1,0:T(1,128)S(1)} async-done(((f32[16,1,256]{2,1,0:T(1,128)}), f32[16,1,256]{2,1,0:T(1,128)S(1)}, u32[]{:S(2)}, u32[]{:S(2)}) %all-to-all-start.3) | async-done | bytes 16416 | tf_op jit(solution)/shard_map/all_to_all | solution.py:199
  104.1 3.5 %collective-permute-done.11 = f32[128,256]{1,0:T(8,128)S(1)} collective-permute-done((f32[128,256]{1,0:T(8,128)S(1)}, f32[128,256]{1,0:T(8,128)S(1)}, u32[]{:S(2)}, u32[]{:S(2)}) %collective-permute-start.11) | collective-permute-done | bytes 131104 | tf_op jit(solution)/shard_map/ppermute | solution.py:215
  107.7 2.5 %collective-permute-start.15 = (f32[128,256]{1,0:T(8,128)S(1)}, f32[128,256]{1,0:T(8,128)S(1)}, u32[]{:S(2)}, u32[]{:S(2)}) collective-permute-start(f32[128,256]{1,0:T(8,128)S(1)} %add_add_fusion.1), channel_id=1, source_target_pairs={{0,6},{2,0},{4,2},{6,4},{8,14},{10,8},{12,10},{14,12},{16,22},{18,... | collective-permute-start | bytes 393224 | tf_op jit(solution)/shard_map/ppermute | solution.py:215
  110.2 1.8 %collective-permute-start.13 = (f32[128,256]{1,0:T(8,128)S(1)}, f32[128,256]{1,0:T(8,128)S(1)}, u32[]{:S(2)}, u32[]{:S(2)}) collective-permute-start(f32[128,256]{1,0:T(8,128)S(1)} %add_add_fusion.1), channel_id=1, source_target_pairs={{0,4},{2,6},{4,0},{6,2},{8,12},{10,14},{12,8},{14,10},{16,20},{18,... | collective-permute-start | bytes 393224 | tf_op jit(solution)/shard_map/ppermute | solution.py:215
  112.0 8.5 %third.1 = f32[64,8,128]{2,1,0:T(8,128)} custom-call(bf16[256,128,256]{2,1,0:T(8,128)(2,1)} %t_ref.5, f32[256,256]{1,0:T(8,128)S(1)} %broadcast_divide_fusion.a_ref, f32[128,256]{1,0:T(8,128)S(1)} %broadcast_divide_fusion.1.b_ref), custom_call_target="tpu_custom_call" | custom-call | flops 4294967296 | bytes 16777216 | tf_op jit(solution)/shard_map/third/pallas_call | solution.py:316
  120.6 3.7 %collective-permute-start.16 = (f32[128,256]{1,0:T(8,128)S(1)}, f32[128,256]{1,0:T(8,128)S(1)}, u32[]{:S(2)}, u32[]{:S(2)}) collective-permute-start(f32[128,256]{1,0:T(8,128)S(1)} %add_add_fusion), channel_id=1, source_target_pairs={{0,32},{32,0},{64,96},{96,64},{1,33},{33,1},{65,97},{97,65},{2,34}... | collective-permute-start | bytes 393224 | tf_op jit(solution)/shard_map/ppermute | solution.py:221
  124.3 4.2 %all-to-all-start.4 = ((f32[64,8,128]{2,1,0:T(8,128)}), f32[64,8,128]{2,1,0:T(8,128)S(1)}, u32[]{:S(2)}, u32[]{:S(2)}) async-start(f32[64,8,128]{2,1,0:T(8,128)} %third.1), calls=%async_computation.4 | async-start | bytes 524288 | tf_op jit(solution)/shard_map/all_to_all | solution.py:193
  128.6 6.0 %inverse.6.rest_0_ = f32[256,256]{1,0:T(8,128)S(1)} custom-call(f32[256,256]{1,0:T(8,128)S(1)} %get-tuple-element.22.one_ref, f32[256,256]{1,0:T(8,128)S(1)} %pad_maximum_fusion.1.two_ref), custom_call_target="tpu_custom_call" | custom-call | flops 8589934592 | bytes 786432 | tf_op jit(solution)/shard_map/inverse/pallas_call | solution.py:176
  134.6 3.2 %all-to-all-done.4 = f32[64,8,128]{2,1,0:T(8,128)S(1)} async-done(((f32[64,8,128]{2,1,0:T(8,128)}), f32[64,8,128]{2,1,0:T(8,128)S(1)}, u32[]{:S(2)}, u32[]{:S(2)}) %all-to-all-start.4) | async-done | bytes 262176 | tf_op jit(solution)/shard_map/all_to_all | solution.py:193
  138.7 6.7 %all-to-all-start.5 = ((f32[128,8,128]{2,1,0:T(8,128)}), f32[128,8,128]{2,1,0:T(8,128)S(1)}, u32[]{:S(2)}, u32[]{:S(2)}) async-start(f32[128,8,128]{2,1,0:T(8,128)} %broadcast_in_dim.13), calls=%async_computation.5 | async-start | bytes 1048576 | tf_op jit(solution)/shard_map/all_to_all | solution.py:199
  145.4 5.8 %inverse.7 = f32[256,256]{1,0:T(8,128)S(1)} custom-call(f32[256,256]{1,0:T(8,128)S(1)} %get-tuple-element.22.one_ref, f32[256,256]{1,0:T(8,128)S(1)} %pad_maximum_fusion.1.two_ref, f32[256,256]{1,0:T(8,128)S(1)} %inverse.6.rest_0_), custom_call_target="tpu_custom_call" | custom-call | flops 8589934592 | bytes 786432 | tf_op jit(solution)/shard_map/inverse/pallas_call | solution.py:176
  151.3 8.2 %all-to-all-done.5 = f32[128,8,128]{2,1,0:T(8,128)S(1)} async-done(((f32[128,8,128]{2,1,0:T(8,128)}), f32[128,8,128]{2,1,0:T(8,128)S(1)}, u32[]{:S(2)}, u32[]{:S(2)}) %all-to-all-start.5) | async-done | bytes 524320 | tf_op jit(solution)/shard_map/all_to_all | solution.py:199
  (59 shorter events, 8.1 us)
Async XLA Ops:
  0.6 30.8 %copy-start = (f32[256,256]{1,0:T(8,128)S(1)}, f32[256,256]{1,0:T(8,128)}, u32[]{:S(2)}) copy-start(f32[256,256]{1,0:T(8,128)} %c_ref.3) | copy-start | bytes 786436
  2.0 14.8 %collective-permute-start.2 = (f32[128,256]{1,0:T(8,128)S(1)}, f32[128,256]{1,0:T(8,128)S(1)}, u32[]{:S(2)}, u32[]{:S(2)}) collective-permute-start(f32[128,256]{1,0:T(8,128)S(1)} %fusion.6), channel_id=1, source_target_pairs={{0,24},{2,26},{4,28},{6,30},{8,0},{10,2},{12,4},{14,6},{16,8},{18,... | collective-permute-start | bytes 393224 | tf_op jit(solution)/shard_map/ppermute | solution.py:215
  6.6 10.1 %collective-permute-start.1 = (f32[128,256]{1,0:T(8,128)S(1)}, f32[128,256]{1,0:T(8,128)S(1)}, u32[]{:S(2)}, u32[]{:S(2)}) collective-permute-start(f32[128,256]{1,0:T(8,128)S(1)} %fusion.6), channel_id=1, source_target_pairs={{0,8},{2,10},{4,12},{6,14},{8,16},{10,18},{12,20},{14,22},{16,24},... | collective-permute-start | bytes 393224 | tf_op jit(solution)/shard_map/ppermute | solution.py:215
  6.6 10.1 %collective-permute-start = (f32[128,256]{1,0:T(8,128)S(1)}, f32[128,256]{1,0:T(8,128)S(1)}, u32[]{:S(2)}, u32[]{:S(2)}) collective-permute-start(f32[128,256]{1,0:T(8,128)S(1)} %fusion.6), channel_id=1, source_target_pairs={{0,16},{2,18},{4,20},{6,22},{8,24},{10,26},{12,28},{14,30},{16,0},... | collective-permute-start | bytes 393224 | tf_op jit(solution)/shard_map/ppermute | solution.py:215
  16.8 11.9 %collective-permute-start.5 = (f32[128,256]{1,0:T(8,128)S(1)}, f32[128,256]{1,0:T(8,128)S(1)}, u32[]{:S(2)}, u32[]{:S(2)}) collective-permute-start(f32[128,256]{1,0:T(8,128)S(1)} %add_add_fusion.3), channel_id=1, source_target_pairs={{0,6},{2,0},{4,2},{6,4},{8,14},{10,8},{12,10},{14,12},{16,22},{18,... | collective-permute-start | bytes 393224 | tf_op jit(solution)/shard_map/ppermute | solution.py:215
  19.6 9.1 %collective-permute-start.4 = (f32[128,256]{1,0:T(8,128)S(1)}, f32[128,256]{1,0:T(8,128)S(1)}, u32[]{:S(2)}, u32[]{:S(2)}) collective-permute-start(f32[128,256]{1,0:T(8,128)S(1)} %add_add_fusion.3), channel_id=1, source_target_pairs={{0,2},{2,4},{4,6},{6,0},{8,10},{10,12},{12,14},{14,8},{16,18},{18,... | collective-permute-start | bytes 393224 | tf_op jit(solution)/shard_map/ppermute | solution.py:215
  19.6 9.1 %collective-permute-start.3 = (f32[128,256]{1,0:T(8,128)S(1)}, f32[128,256]{1,0:T(8,128)S(1)}, u32[]{:S(2)}, u32[]{:S(2)}) collective-permute-start(f32[128,256]{1,0:T(8,128)S(1)} %add_add_fusion.3), channel_id=1, source_target_pairs={{0,4},{2,6},{4,0},{6,2},{8,12},{10,14},{12,8},{14,10},{16,20},{18,... | collective-permute-start | bytes 393224 | tf_op jit(solution)/shard_map/ppermute | solution.py:215
  21.2 17.3 %all-to-all-start = ((f32[32,8,256]{2,1,0:T(8,128)}), f32[32,8,256]{2,1,0:T(8,128)S(1)}, u32[]{:S(2)}, u32[]{:S(2)}) async-start(f32[32,8,256]{2,1,0:T(8,128)} %bitcast.20), calls=%async_computation | async-start | bytes 524288 | tf_op jit(solution)/shard_map/all_to_all | solution.py:193
  28.7 14.5 %collective-permute-start.6 = (f32[128,256]{1,0:T(8,128)S(1)}, f32[128,256]{1,0:T(8,128)S(1)}, u32[]{:S(2)}, u32[]{:S(2)}) collective-permute-start(f32[128,256]{1,0:T(8,128)S(1)} %add_add_fusion.2), channel_id=1, source_target_pairs={{0,32},{32,0},{64,96},{96,64},{1,33},{33,1},{65,97},{97,65},{2,34}... | collective-permute-start | bytes 393224 | tf_op jit(solution)/shard_map/ppermute | solution.py:221
  32.1 11.2 %collective-permute-start.7 = (f32[256,256]{1,0:T(8,128)S(1)}, f32[256,256]{1,0:T(8,128)S(1)}, u32[]{:S(2)}, u32[]{:S(2)}) collective-permute-start(f32[256,256]{1,0:T(8,128)S(1)} %fusion.11), channel_id=1, source_target_pairs={{0,1},{1,0},{2,3},{3,2},{4,5},{5,4},{6,7},{7,6},{8,9},{9,8},{10,11... | collective-permute-start | bytes 786440 | tf_op jit(solution)/shard_map/ppermute | solution.py:204
  39.3 15.5 %all-to-all-start.1 = ((f32[32,8,256]{2,1,0:T(8,128)}), f32[32,8,256]{2,1,0:T(8,128)S(1)}, u32[]{:S(2)}, u32[]{:S(2)}) async-start(f32[32,8,256]{2,1,0:T(8,128)} %broadcast_in_dim.10), calls=%async_computation.1 | async-start | bytes 524288 | tf_op jit(solution)/shard_map/all_to_all | solution.py:199
  55.8 13.4 %collective-permute-start.8 = (f32[256,256]{1,0:T(8,128)S(1)}, f32[256,256]{1,0:T(8,128)S(1)}, u32[]{:S(2)}, u32[]{:S(2)}) collective-permute-start(f32[256,256]{1,0:T(8,128)S(1)} %fusion.12), channel_id=1, source_target_pairs={{0,32},{32,0},{64,96},{96,64},{1,33},{33,1},{65,97},{97,65},{2,34}... | collective-permute-start | bytes 786440 | tf_op jit(solution)/shard_map/ppermute | solution.py:204
  69.2 8.0 %collective-permute-start.9 = (f32[256,256]{1,0:T(8,128)S(1)}, f32[256,256]{1,0:T(8,128)S(1)}, u32[]{:S(2)}, u32[]{:S(2)}) collective-permute-start(f32[256,256]{1,0:T(8,128)S(1)} %add.94), channel_id=1, source_target_pairs={{0,64},{32,96},{64,0},{96,32},{1,65},{33,97},{65,1},{97,33},{2,66}... | collective-permute-start | bytes 786440 | tf_op jit(solution)/shard_map/ppermute | solution.py:204
  69.7 20.3 %all-to-all-start.2 = ((f32[8,128,256]{2,1,0:T(8,128)}), f32[8,128,256]{2,1,0:T(8,128)S(1)}, u32[]{:S(2)}, u32[]{:S(2)}) async-start(f32[8,128,256]{2,1,0:T(8,128)} %second.1), calls=%async_computation.2 | async-start | bytes 2097152 | tf_op jit(solution)/shard_map/all_to_all | solution.py:364
  88.8 45.8 %copy-start.1 = (f32[256,256]{1,0:T(8,128)}, f32[256,256]{1,0:T(8,128)S(1)}, u32[]{:S(2)}) copy-start(f32[256,256]{1,0:T(8,128)S(1)} %broadcast_divide_fusion.a_ref) | copy-start | bytes 786436
  91.0 13.1 %all-to-all-start.3 = ((f32[16,1,256]{2,1,0:T(1,128)}), f32[16,1,256]{2,1,0:T(1,128)S(1)}, u32[]{:S(2)}, u32[]{:S(2)}) async-start(f32[16,1,256]{2,1,0:T(1,128)} %broadcast_in_dim.12), calls=%async_computation.3 | async-start | bytes 32768 | tf_op jit(solution)/shard_map/all_to_all | solution.py:199
  97.9 6.2 %collective-permute-start.12 = (f32[128,256]{1,0:T(8,128)S(1)}, f32[128,256]{1,0:T(8,128)S(1)}, u32[]{:S(2)}, u32[]{:S(2)}) collective-permute-start(f32[128,256]{1,0:T(8,128)S(1)} %fusion.4), channel_id=1, source_target_pairs={{0,24},{2,26},{4,28},{6,30},{8,0},{10,2},{12,4},{14,6},{16,8},{18,... | collective-permute-start | bytes 393224 | tf_op jit(solution)/shard_map/ppermute | solution.py:215
  100.6 7.1 %collective-permute-start.11 = (f32[128,256]{1,0:T(8,128)S(1)}, f32[128,256]{1,0:T(8,128)S(1)}, u32[]{:S(2)}, u32[]{:S(2)}) collective-permute-start(f32[128,256]{1,0:T(8,128)S(1)} %fusion.4), channel_id=1, source_target_pairs={{0,8},{2,10},{4,12},{6,14},{8,16},{10,18},{12,20},{14,22},{16,24},... | collective-permute-start | bytes 393224 | tf_op jit(solution)/shard_map/ppermute | solution.py:215
  100.6 7.1 %collective-permute-start.10 = (f32[128,256]{1,0:T(8,128)S(1)}, f32[128,256]{1,0:T(8,128)S(1)}, u32[]{:S(2)}, u32[]{:S(2)}) collective-permute-start(f32[128,256]{1,0:T(8,128)S(1)} %fusion.4), channel_id=1, source_target_pairs={{0,16},{2,18},{4,20},{6,22},{8,24},{10,26},{12,28},{14,30},{16,0},... | collective-permute-start | bytes 393224 | tf_op jit(solution)/shard_map/ppermute | solution.py:215
  104.1 30.5 %copy-start.2 = (f32[128,256]{1,0:T(8,128)}, f32[128,256]{1,0:T(8,128)S(1)}, u32[]{:S(2)}) copy-start(f32[128,256]{1,0:T(8,128)S(1)} %broadcast_divide_fusion.1.b_ref) | copy-start | bytes 393220
  107.7 12.8 %collective-permute-start.15 = (f32[128,256]{1,0:T(8,128)S(1)}, f32[128,256]{1,0:T(8,128)S(1)}, u32[]{:S(2)}, u32[]{:S(2)}) collective-permute-start(f32[128,256]{1,0:T(8,128)S(1)} %add_add_fusion.1), channel_id=1, source_target_pairs={{0,6},{2,0},{4,2},{6,4},{8,14},{10,8},{12,10},{14,12},{16,22},{18,... | collective-permute-start | bytes 393224 | tf_op jit(solution)/shard_map/ppermute | solution.py:215
  110.2 10.3 %collective-permute-start.14 = (f32[128,256]{1,0:T(8,128)S(1)}, f32[128,256]{1,0:T(8,128)S(1)}, u32[]{:S(2)}, u32[]{:S(2)}) collective-permute-start(f32[128,256]{1,0:T(8,128)S(1)} %add_add_fusion.1), channel_id=1, source_target_pairs={{0,2},{2,4},{4,6},{6,0},{8,10},{10,12},{12,14},{14,8},{16,18},{18,... | collective-permute-start | bytes 393224 | tf_op jit(solution)/shard_map/ppermute | solution.py:215
  110.2 10.3 %collective-permute-start.13 = (f32[128,256]{1,0:T(8,128)S(1)}, f32[128,256]{1,0:T(8,128)S(1)}, u32[]{:S(2)}, u32[]{:S(2)}) collective-permute-start(f32[128,256]{1,0:T(8,128)S(1)} %add_add_fusion.1), channel_id=1, source_target_pairs={{0,4},{2,6},{4,0},{6,2},{8,12},{10,14},{12,8},{14,10},{16,20},{18,... | collective-permute-start | bytes 393224 | tf_op jit(solution)/shard_map/ppermute | solution.py:215
  120.6 7.9 %collective-permute-start.16 = (f32[128,256]{1,0:T(8,128)S(1)}, f32[128,256]{1,0:T(8,128)S(1)}, u32[]{:S(2)}, u32[]{:S(2)}) collective-permute-start(f32[128,256]{1,0:T(8,128)S(1)} %add_add_fusion), channel_id=1, source_target_pairs={{0,32},{32,0},{64,96},{96,64},{1,33},{33,1},{65,97},{97,65},{2,34}... | collective-permute-start | bytes 393224 | tf_op jit(solution)/shard_map/ppermute | solution.py:221
  124.3 13.5 %all-to-all-start.4 = ((f32[64,8,128]{2,1,0:T(8,128)}), f32[64,8,128]{2,1,0:T(8,128)S(1)}, u32[]{:S(2)}, u32[]{:S(2)}) async-start(f32[64,8,128]{2,1,0:T(8,128)} %third.1), calls=%async_computation.4 | async-start | bytes 524288 | tf_op jit(solution)/shard_map/all_to_all | solution.py:193
  138.7 20.8 %all-to-all-start.5 = ((f32[128,8,128]{2,1,0:T(8,128)}), f32[128,8,128]{2,1,0:T(8,128)S(1)}, u32[]{:S(2)}, u32[]{:S(2)}) async-start(f32[128,8,128]{2,1,0:T(8,128)} %broadcast_in_dim.13), calls=%async_computation.5 | async-start | bytes 1048576 | tf_op jit(solution)/shard_map/all_to_all | solution.py:199
